TPU v7x, 32 devices: a whole 2x2x4 slice. The times are simulated.
32 devices in a mesh: node: 16 (over z, x, core), feat: 2 (over y).
Axes of the slice: x: 2, y: 2, z: 4, core: 2. Of those that a mesh axis runs over, the one named last changes fastest.
Arguments:
- grid_in: bfloat16 [3, 4096, 227], P(None, ('node', 'feat')), may hold values from -6 to 6
- targets: bfloat16 [3, 4096, 83], P(None, ('node', 'feat')), may hold values from -6 to 6
- area: float32 [4096], P(('node', 'feat')), as said below
- row_count: int32 [3, 32], P(None, ('node', 'feat')), may hold values from 64 to 128, as said below
- g2m: int32 [4096, 8], P('node'), may hold values from 0 to 255
- m2g: int32 [4096, 3], P('node'), may hold values from 0 to 255
- senders: int32 [4096, 16], P('node'), may hold values from 0 to 511
- edge_count: int32 [32], P('node'), may hold values from 4 to 16, as said below
- mat_w: float32 [12, 512, 512], P(None, ('node', 'feat')), may hold values from -0.25 to 0.25
- mat_m: float32 [12, 512, 512], P(None, ('node', 'feat')), may hold values from -0.00015258789 to 0.00015258789
- mat_v: float32 [12, 512, 512], P(None, ('node', 'feat')), may hold values from 7.553856e-10 to 3.0215423e-09
- in_w: float32 [227, 512], P(None, ('node', 'feat')), may hold values from -0.375 to 0.375
- in_m: float32 [227, 512], P(None, ('node', 'feat')), may hold values from -0.00015258789 to 0.00015258789
- in_v: float32 [227, 512], P(None, ('node', 'feat')), may hold values from 7.553856e-10 to 3.0215423e-09
- out_w: float32 [512, 83], P(('node', 'feat')), may hold values from -0.25 to 0.25
- out_m: float32 [512, 83], P(('node', 'feat')), may hold values from -0.00015258789 to 0.00015258789
- out_v: float32 [512, 83], P(('node', 'feat')), may hold values from 7.553856e-10 to 3.0215423e-09
- gain_w: float32 [5, 512], P(None, ('node', 'feat')), may hold values from 0.5 to 1.5
- gain_m: float32 [5, 512], P(None, ('node', 'feat')), may hold values from -0.00061035156 to 0.00061035156
- gain_v: float32 [5, 512], P(None, ('node', 'feat')), may hold values from 3.0215423e-09 to 4.8344678e-08
- bias_w: float32 [5, 512], P(None, ('node', 'feat')), may hold values from -2 to 2
- bias_m: float32 [5, 512], P(None, ('node', 'feat')), may hold values from -0.00061035156 to 0.00061035156
- bias_v: float32 [5, 512], P(None, ('node', 'feat')), may hold values from 3.0215423e-09 to 4.8344678e-08
Outputs:
- mat_new: float32 [12, 512, 512], P(None, ('node', 'feat'))
- mat_first: float32 [12, 512, 512], P(None, ('node', 'feat'))
- mat_second: float32 [12, 512, 512], P(None, ('node', 'feat'))
- mat_copy: bfloat16 [12, 512, 512], P(None, ('node', 'feat'))
- in_new: float32 [227, 512], P(None, ('node', 'feat'))
- in_first: float32 [227, 512], P(None, ('node', 'feat'))
- in_second: float32 [227, 512], P(None, ('node', 'feat'))
- in_copy: bfloat16 [227, 512], P(None, ('node', 'feat'))
- out_new: float32 [512, 83], P(('node', 'feat'))
- out_first: float32 [512, 83], P(('node', 'feat'))
- out_second: float32 [512, 83], P(('node', 'feat'))
- out_copy: bfloat16 [512, 83], P(('node', 'feat'))
- gain_new: float32 [5, 512], P(None, ('node', 'feat'))
- gain_first: float32 [5, 512], P(None, ('node', 'feat'))
- gain_second: float32 [5, 512], P(None, ('node', 'feat'))
- gain_copy: bfloat16 [5, 512], P(None, ('node', 'feat'))
- bias_new: float32 [5, 512], P(None, ('node', 'feat'))
- bias_first: float32 [5, 512], P(None, ('node', 'feat'))
- bias_second: float32 [5, 512], P(None, ('node', 'feat'))
- bias_copy: bfloat16 [5, 512], P(None, ('node', 'feat'))
- loss_sum: float32 [], replicated
- weight_total: float32 [], replicated
- grad_norm: float32 [], replicated
Inputs may be any that keep to these rules, and one draw needn't show every extreme that they name: `row_count`: each device's count of live grid rows in a micro-batch; some device has all. `edge_count`: live slots of an adjacency block; some block has all. `area`: positive; padded rows are those beyond row_count.
All inputs are finite; a program needn't handle non-finite values.
Results may differ from a plain program's by a relative error of at most 0.002.
Values may be sent and summed in bfloat16 or wider, within the bound.
A program may use at most 256 MiB of HBM per device.

v0:
```python
import jax
import jax.numpy as jnp
from jax import lax
from jax.sharding import PartitionSpec as P

HEADS = 8
STEP = 5


NORM_EPS = 1e-05
CLIP = 0.05
RATE = 0.02
BETA_ONE = 0.5
BETA_TWO = 0.5
DECAY = 0.01
ADAM_EPS = 1e-08
MASKED = -1000000000.0


def passed_along(value, axis, steps):
    count = lax.axis_size(axis)
    pairs = [(source, (source + steps) % count) for source in range(count)]
    return lax.ppermute(value, axis, pairs)


def product(left, right):
    return jnp.dot(left, right, preferred_element_type=jnp.float32)


def product_left(left, right):
    return lax.dot_general(
        left, right, (((0,), (0,)), ((), ())), preferred_element_type=jnp.float32
    )


def product_right(left, right):
    return lax.dot_general(
        left, right, (((1,), (1,)), ((), ())), preferred_element_type=jnp.float32
    )


def layer_norm(state, gain):
    centre = state - jnp.mean(state, axis=-1, keepdims=True)
    spread = jnp.mean(centre * centre, axis=-1, keepdims=True)
    return centre * lax.rsqrt(spread + NORM_EPS) * gain


def to_columns(stacked):
    return lax.all_to_all(stacked, "feat", split_axis=2, concat_axis=1, tiled=True)


def to_rows(stacked):
    return lax.all_to_all(stacked, "feat", split_axis=1, concat_axis=2, tiled=True)


def spread_rows(grad, index, count):
    slots = index.shape[1]
    copies = jnp.broadcast_to(grad[:, None, :] / slots, (grad.shape[0], slots, grad.shape[1]))
    return jax.ops.segment_sum(
        copies.reshape(-1, grad.shape[1]), index.reshape(-1), num_segments=count
    )


def fetch_all(mat_w, in_w, out_w, gain_w, bias_w):
    return (
        lax.all_gather(mat_w.astype(jnp.bfloat16), ("node", "feat"), axis=1, tiled=True),
        lax.all_gather(in_w.astype(jnp.bfloat16), ("node", "feat"), axis=1, tiled=True),
        lax.all_gather(out_w.astype(jnp.bfloat16), ("node", "feat"), axis=0, tiled=True),
        lax.all_gather(gain_w.astype(jnp.bfloat16), ("node", "feat"), axis=1, tiled=True),
        lax.all_gather(bias_w.astype(jnp.bfloat16), ("node", "feat"), axis=1, tiled=True),
    )


def reduce_grads(grad_mats, grad_in, grad_out, grad_gain, grad_bias):
    return (
        lax.psum_scatter(grad_mats, ("node", "feat"), scatter_dimension=1, tiled=True),
        lax.psum_scatter(grad_in, ("node", "feat"), scatter_dimension=1, tiled=True),
        lax.psum_scatter(grad_out, ("node", "feat"), scatter_dimension=0, tiled=True),
        lax.psum_scatter(grad_gain, ("node", "feat"), scatter_dimension=1, tiled=True),
        lax.psum_scatter(grad_bias, ("node", "feat"), scatter_dimension=1, tiled=True),
    )


def gather_edges(queries, keys_all, values_all, senders, head_count):
    row_total, col_total = queries.shape
    width = col_total // head_count
    keys_per_edge = jnp.take(keys_all, senders, axis=0).reshape(row_total, -1, head_count, width)
    values_per_edge = jnp.take(values_all, senders, axis=0).reshape(
        row_total, -1, head_count, width
    )
    return (
        queries.reshape(row_total, head_count, width),
        keys_per_edge,
        values_per_edge,
        width ** (-0.5),
    )


def attend(queries, keys_all, values_all, senders, allowed, head_count):
    query_per_head, keys_per_edge, values_per_edge, scale = gather_edges(
        queries, keys_all, values_all, senders, head_count
    )
    edge_scores = (
        jnp.einsum(
            "lgz,lpgz->lgp", query_per_head, keys_per_edge, preferred_element_type=jnp.float32
        )
        * scale
    )
    edge_scores = jnp.where(allowed[:, None, :], edge_scores, MASKED)
    expo = jnp.exp(edge_scores - jnp.max(edge_scores, axis=-1, keepdims=True))
    attention_probabilities = expo / jnp.sum(expo, axis=-1, keepdims=True)
    mixed_values = jnp.einsum(
        "vzn,vnzb->vzb",
        attention_probabilities.astype(jnp.bfloat16),
        values_per_edge,
        preferred_element_type=jnp.float32,
    )
    return (mixed_values.reshape(queries.shape).astype(jnp.bfloat16), attention_probabilities)


def attend_back(
    grad_mixed, queries, keys_all, values_all, senders, attention_probabilities, head_count
):
    query_per_head, keys_per_edge, values_per_edge, scale = gather_edges(
        queries, keys_all, values_all, senders, head_count
    )
    row_total, col_total = queries.shape
    gradient_per_head = grad_mixed.reshape(row_total, head_count, -1)
    grad_probs = jnp.einsum(
        "lgz,lpgz->lgp", gradient_per_head, values_per_edge, preferred_element_type=jnp.float32
    )
    grad_values = jnp.einsum(
        "yvz,yvs->yzvs",
        attention_probabilities.astype(jnp.bfloat16),
        gradient_per_head,
        preferred_element_type=jnp.float32,
    )
    grad_scores = attention_probabilities * (
        grad_probs - jnp.sum(attention_probabilities * grad_probs, axis=-1, keepdims=True)
    )
    scores_reduced = grad_scores.astype(jnp.bfloat16)
    grad_queries = scale * jnp.einsum(
        "vzn,vnzb->vzb", scores_reduced, keys_per_edge, preferred_element_type=jnp.float32
    )
    grad_keys = scale * jnp.einsum(
        "yvz,yvs->yzvs", scores_reduced, query_per_head, preferred_element_type=jnp.float32
    )
    count = keys_all.shape[0]
    flat_ids = senders.reshape(-1)
    keys_sum = jax.ops.segment_sum(grad_keys.reshape(-1, col_total), flat_ids, num_segments=count)
    values_sum = jax.ops.segment_sum(
        grad_values.reshape(-1, col_total), flat_ids, num_segments=count
    )
    return (grad_queries.reshape(row_total, col_total), keys_sum, values_sum)


def layer_forward(state, mats, gains, biases, layer, senders, allowed, head_count):
    base = 6 * layer
    gain_attn = gains[2 * layer].astype(jnp.float32)
    gain_mlp = gains[2 * layer + 1].astype(jnp.float32)
    normed = layer_norm(state, gain_attn).astype(jnp.bfloat16)
    projected = jnp.einsum(
        "rd,kde->kre", normed, mats[base : base + 3], preferred_element_type=jnp.float32
    )
    qkv_cols = to_columns(projected.astype(jnp.bfloat16))
    mesh_rows = qkv_cols.shape[1]
    before = passed_along(qkv_cols[1:], "node", 1)
    keys_all = jnp.concatenate([qkv_cols[1], before[0]], axis=0)
    values_all = jnp.concatenate([qkv_cols[2], before[1]], axis=0)
    mixed_values, attention_probabilities = attend(
        qkv_cols[0], keys_all, values_all, senders, allowed, head_count
    )
    mixed_rows = to_rows(mixed_values[None])[0]
    middle = state + product(mixed_rows, mats[base + 3])
    normed_mlp = layer_norm(middle, gain_mlp).astype(jnp.bfloat16)
    pre_mlp = product(normed_mlp, mats[base + 4]) + biases[1 + 2 * layer].astype(jnp.float32)
    hidden = jax.nn.silu(pre_mlp).astype(jnp.bfloat16)
    result = middle + product(hidden, mats[base + 5]) + biases[2 + 2 * layer].astype(jnp.float32)
    kept = (
        state,
        gain_attn,
        gain_mlp,
        normed,
        qkv_cols,
        keys_all,
        values_all,
        attention_probabilities,
        mixed_rows,
        middle,
        normed_mlp,
        pre_mlp,
        hidden,
        mesh_rows,
    )
    return (result, kept)


def layer_backward(grad, kept, mats, layer, senders, head_count):
    (
        state,
        gain_attn,
        gain_mlp,
        normed,
        qkv_cols,
        keys_all,
        values_all,
        attention_probabilities,
        mixed_rows,
        middle,
        normed_mlp,
        pre_mlp,
        hidden,
        mesh_rows,
    ) = kept
    base = 6 * layer
    grad_low = grad.astype(jnp.bfloat16)
    grad_second = product_left(hidden, grad_low)
    bias_second = jnp.sum(grad, axis=0)
    grad_hidden = product_right(grad_low, mats[base + 5])
    grad_pre = jax.vjp(jax.nn.silu, pre_mlp)[1](grad_hidden)[0].astype(jnp.bfloat16)
    bias_first = jnp.sum(grad_pre.astype(jnp.float32), axis=0)
    grad_first = product_left(normed_mlp, grad_pre)
    grad_normed = product_right(grad_pre, mats[base + 4])
    grad_mid, gain_mlp_grad = jax.vjp(layer_norm, middle, gain_mlp)[1](grad_normed)
    grad_mid = grad_mid + grad
    mid_low = grad_mid.astype(jnp.bfloat16)
    grad_output = product_left(mixed_rows, mid_low)
    grad_mixed = product_right(mid_low, mats[base + 3]).astype(jnp.bfloat16)
    grad_cols = to_columns(grad_mixed[None])[0]
    grad_queries, keys_sum, values_sum = attend_back(
        grad_cols, qkv_cols[0], keys_all, values_all, senders, attention_probabilities, head_count
    )
    returned = passed_along(
        jnp.stack([keys_sum[mesh_rows:], values_sum[mesh_rows:]]).astype(jnp.bfloat16), "node", -1
    ).astype(jnp.float32)
    stacked = jnp.stack(
        [grad_queries, keys_sum[:mesh_rows] + returned[0], values_sum[:mesh_rows] + returned[1]]
    ).astype(jnp.bfloat16)
    grad_proj = to_rows(stacked)
    grad_qkv = jnp.einsum("rd,kre->kde", normed, grad_proj, preferred_element_type=jnp.float32)
    grad_norm_in = jnp.einsum(
        "kre,kde->rd", grad_proj, mats[base : base + 3], preferred_element_type=jnp.float32
    )
    grad_state, gain_attn_grad = jax.vjp(layer_norm, state, gain_attn)[1](grad_norm_in)
    grad_mats = jnp.concatenate(
        [grad_qkv, grad_output[None], grad_first[None], grad_second[None]], axis=0
    )
    return (
        grad_state + grad_mid,
        (grad_mats, gain_attn_grad, gain_mlp_grad, bias_first, bias_second),
    )


def micro_step(full, grid_rows, target, wrow, weight_total, g2m, m2g, senders, allowed, head_count):
    mats, inputs, outputs, gains, biases = full
    layer_total = mats.shape[0] // 6
    mesh_rows = g2m.shape[0]
    group_rows = m2g.shape[0]
    pre_enc = product(grid_rows, inputs) + biases[0].astype(jnp.float32)
    encoded = jax.nn.silu(pre_enc).astype(jnp.bfloat16)
    enc_cols = to_columns(encoded[None])[0]
    start_cols = jnp.mean(jnp.take(enc_cols, g2m, axis=0).astype(jnp.float32), axis=1).astype(
        jnp.bfloat16
    )
    state = to_rows(start_cols[None])[0].astype(jnp.float32)
    kept_all = []
    for layer in range(layer_total):
        state, kept = layer_forward(state, mats, gains, biases, layer, senders, allowed, head_count)
        kept_all.append(kept)
    last_cols = to_columns(state.astype(jnp.bfloat16)[None])[0]
    decoded = jnp.mean(jnp.take(last_cols, m2g, axis=0).astype(jnp.float32), axis=1).astype(
        jnp.bfloat16
    )
    dec_rows = to_rows(decoded[None])[0].astype(jnp.float32)
    gain_dec = gains[2 * layer_total].astype(jnp.float32)
    final_normed = layer_norm(dec_rows, gain_dec).astype(jnp.bfloat16)
    predict = product(final_normed, outputs)
    error = predict - target.astype(jnp.float32)
    loss_part = jnp.sum(wrow[:, None] * error * error)
    grad_pred = (2.0 * wrow[:, None] * error / weight_total).astype(jnp.bfloat16)
    back_mats, back_out = (mats, outputs)
    grad_out = product_left(final_normed, grad_pred)
    grad_final = product_right(grad_pred, back_out)
    grad_dec, gain_dec_grad = jax.vjp(layer_norm, dec_rows, gain_dec)[1](grad_final)
    grad_dec_cols = to_columns(grad_dec.astype(jnp.bfloat16)[None])[0].astype(jnp.float32)
    grad_last = spread_rows(grad_dec_cols, m2g, mesh_rows)
    grad_state = to_rows(grad_last.astype(jnp.bfloat16)[None])[0].astype(jnp.float32)
    mat_parts = []
    gain_parts = []
    bias_parts = []
    for layer in reversed(range(layer_total)):
        grad_state, pieces = layer_backward(
            grad_state, kept_all[layer], back_mats, layer, senders, head_count
        )
        mat_parts.insert(0, pieces[0])
        gain_parts = [pieces[1], pieces[2]] + gain_parts
        bias_parts = [pieces[3], pieces[4]] + bias_parts
    grad_start = to_columns(grad_state.astype(jnp.bfloat16)[None])[0].astype(jnp.float32)
    grad_enc = spread_rows(grad_start, g2m, group_rows)
    grad_enc_rows = to_rows(grad_enc.astype(jnp.bfloat16)[None])[0].astype(jnp.float32)
    grad_pre_enc = jax.vjp(jax.nn.silu, pre_enc)[1](grad_enc_rows)[0].astype(jnp.bfloat16)
    grad_in = product_left(grid_rows, grad_pre_enc)
    bias_enc = jnp.sum(grad_pre_enc.astype(jnp.float32), axis=0)
    grads = (
        jnp.concatenate(mat_parts, axis=0),
        grad_in,
        grad_out,
        jnp.stack(gain_parts + [gain_dec_grad]),
        jnp.stack([bias_enc] + bias_parts),
    )
    return (loss_part, grads)


def adam(weight, first, second, grad):
    first_new = BETA_ONE * first + (1.0 - BETA_ONE) * grad
    second_new = BETA_TWO * second + (1.0 - BETA_TWO) * grad * grad
    first_hat = first_new / (1.0 - BETA_ONE**STEP)
    second_hat = second_new / (1.0 - BETA_TWO**STEP)
    weight_new = weight - RATE * (first_hat / (jnp.sqrt(second_hat) + ADAM_EPS) + DECAY * weight)
    return (weight_new, first_new, second_new, weight_new.astype(jnp.bfloat16))


def per_device(
    grid_in,
    targets,
    area,
    row_count,
    g2m,
    m2g,
    senders,
    edge_count,
    mat_w,
    mat_m,
    mat_v,
    in_w,
    in_m,
    in_v,
    out_w,
    out_m,
    out_v,
    gain_w,
    gain_m,
    gain_v,
    bias_w,
    bias_m,
    bias_v,
):
    head_count = HEADS // lax.axis_size("feat")
    mesh_rows = g2m.shape[0]
    grid_rows = grid_in.shape[1]
    block_rows = mesh_rows // edge_count.shape[0]
    allowed = jnp.arange(senders.shape[1])[None, :] < jnp.repeat(edge_count, block_rows)[:, None]
    weights_all = area[None, :] * (jnp.arange(grid_rows)[None, :] < row_count).astype(jnp.float32)
    weight_total = lax.psum(jnp.sum(weights_all) * targets.shape[2], ("node", "feat"))
    shard_total = tuple(
        (jnp.zeros(master.shape, jnp.float32) for master in (mat_w, in_w, out_w, gain_w, bias_w))
    )
    loss_local = jnp.float32(0.0)
    for batch in range(grid_in.shape[0]):
        full = fetch_all(mat_w, in_w, out_w, gain_w, bias_w)
        loss_part, grads = micro_step(
            full,
            grid_in[batch],
            targets[batch],
            weights_all[batch],
            weight_total,
            g2m,
            m2g,
            senders,
            allowed,
            head_count,
        )
        loss_local = loss_local + loss_part
        shares = reduce_grads(grads[0], grads[1], grads[2], grads[3], grads[4])
        shard_total = tuple((total_part + extra for total_part, extra in zip(shard_total, shares)))
    squares = jnp.float32(0.0)
    for total_part in shard_total:
        squares = squares + jnp.sum(total_part * total_part)
    square_sum, loss_sum = lax.psum((squares, loss_local), ("node", "feat"))
    grad_norm = jnp.sqrt(square_sum)
    factor = jnp.minimum(1.0, CLIP / (grad_norm + 1e-06))
    mat_new, mat_first, mat_second, mat_copy = adam(mat_w, mat_m, mat_v, factor * shard_total[0])
    in_new, in_first, in_second, in_copy = adam(in_w, in_m, in_v, factor * shard_total[1])
    out_new, out_first, out_second, out_copy = adam(out_w, out_m, out_v, factor * shard_total[2])
    gain_new, gain_first, gain_second, gain_copy = adam(
        gain_w, gain_m, gain_v, factor * shard_total[3]
    )
    bias_new, bias_first, bias_second, bias_copy = adam(
        bias_w, bias_m, bias_v, factor * shard_total[4]
    )
    return (
        mat_new,
        mat_first,
        mat_second,
        mat_copy,
        in_new,
        in_first,
        in_second,
        in_copy,
        out_new,
        out_first,
        out_second,
        out_copy,
        gain_new,
        gain_first,
        gain_second,
        gain_copy,
        bias_new,
        bias_first,
        bias_second,
        bias_copy,
        loss_sum,
        weight_total,
        grad_norm,
    )


def solution(mesh):
    placed = (
        P(None, ("node", "feat"), None),
        P(None, ("node", "feat"), None),
        P(("node", "feat")),
        P(None, ("node", "feat")),
        P("node", None),
        P("node", None),
        P("node", None),
        P("node"),
        P(None, ("node", "feat"), None),
        P(None, ("node", "feat"), None),
        P(None, ("node", "feat"), None),
        P(None, ("node", "feat")),
        P(None, ("node", "feat")),
        P(None, ("node", "feat")),
        P(("node", "feat"), None),
        P(("node", "feat"), None),
        P(("node", "feat"), None),
        P(None, ("node", "feat")),
        P(None, ("node", "feat")),
        P(None, ("node", "feat")),
        P(None, ("node", "feat")),
        P(None, ("node", "feat")),
        P(None, ("node", "feat")),
    )
    return jax.shard_map(
        per_device,
        mesh=mesh,
        in_specs=placed,
        out_specs=(
            P(None, ("node", "feat"), None),
            P(None, ("node", "feat"), None),
            P(None, ("node", "feat"), None),
            P(None, ("node", "feat"), None),
            P(None, ("node", "feat")),
            P(None, ("node", "feat")),
            P(None, ("node", "feat")),
            P(None, ("node", "feat")),
            P(("node", "feat"), None),
            P(("node", "feat"), None),
            P(("node", "feat"), None),
            P(("node", "feat"), None),
            P(None, ("node", "feat")),
            P(None, ("node", "feat")),
            P(None, ("node", "feat")),
            P(None, ("node", "feat")),
            P(None, ("node", "feat")),
            P(None, ("node", "feat")),
            P(None, ("node", "feat")),
            P(None, ("node", "feat")),
            P(),
            P(),
            P(),
        ),
        check_vma=False,
    )
```

profile of v0, /device:TPU:0, one launch (start us, length us, event | category | flops | bytes accessed | tf_op | source)
XLA Modules:
  0.0 2669.4 jit_solution(16207834538755230846)
XLA Ops:
  10.5 70.8 %all-gather = bf16[32,16,5]{1,2,0:T(8,128)(2,1)S(1)} all-gather(bf16[1,16,5]{1,2,0:T(8,128)(2,1)S(1)} %convert_bitcast_fusion.10), channel_id=1, replica_groups=mesh['node'=16,'feat'=2] {'node','feat'}, dimensions={0}, use_global_device_ids=true | all-gather | bytes 5280 | tf_op jit(solution)/shard_map/all_gather | solution.py:70
  81.4 64.7 %all_gather.10 = bf16[227,512]{0,1:T(8,128)(2,1)S(1)} all-gather(bf16[227,16]{0,1:T(8,128)(2,1)S(1)} %convert_element_type.863), channel_id=1, replica_groups=mesh['node'=16,'feat'=2] {'node','feat'}, dimensions={1}, use_global_device_ids=true | all-gather | bytes 239712 | tf_op jit(solution)/shard_map/all_gather | solution.py:67
  155.6 65.8 %all-gather.1 = bf16[32,16,5]{1,2,0:T(8,128)(2,1)S(1)} all-gather(bf16[1,16,5]{1,2,0:T(8,128)(2,1)S(1)} %convert_bitcast_fusion.9), channel_id=1, replica_groups=mesh['node'=16,'feat'=2] {'node','feat'}, dimensions={0}, use_global_device_ids=true | all-gather | bytes 5280 | tf_op jit(solution)/shard_map/all_gather | solution.py:69
  243.9 36.8 %psum.21 = f32[]{:T(128)} all-reduce(f32[]{:T(128)S(6)} %mul.1462), channel_id=1, replica_groups=mesh['node'=16,'feat'=2] {'node','feat'}, use_global_device_ids=true, to_apply=%region_19.23 | all-reduce | flops 1 | bytes 8 | tf_op jit(solution)/shard_map/psum | solution.py:354
  284.9 71.6 %all_gather.14 = bf16[512,83]{1,0:T(8,128)(2,1)} all-gather(bf16[16,83]{1,0:T(8,128)(2,1)S(1)} %convert_element_type.905), channel_id=1, replica_groups=mesh['node'=16,'feat'=2] {'node','feat'}, dimensions={0}, use_global_device_ids=true | all-gather | bytes 87648 | tf_op jit(solution)/shard_map/all_gather | solution.py:68
  452.6 16.9 gather_fusion.2
  473.6 16.9 gather_fusion.1
  558.5 16.9 gather_fusion.7
  578.4 16.9 gather_fusion.13
  599.6 16.9 gather_fusion.14
  622.5 16.9 gather_fusion.4
  643.7 16.9 gather_fusion.3
  804.7 14.6 gather_fusion.10
  1148.7 23.6 scatter_custom_fusion.11
  1189.5 24.0 scatter_custom_fusion.1
  1229.8 23.6 scatter_custom_fusion.6
  1269.7 23.6 scatter_custom_fusion.12
  1310.9 23.6 scatter_custom_fusion.2
  1357.8 23.0 scatter_custom_fusion.7
  1536.9 23.6 scatter_custom_fusion.8
  1577.7 23.8 scatter_custom_fusion.3
  1618.2 23.6 scatter_custom_fusion.13
  1659.0 23.6 scatter_custom_fusion.9
  1701.3 23.6 scatter_custom_fusion.4
  1742.4 23.0 scatter_custom_fusion.14
  1930.4 18.9 add_add_fusion
  1949.3 18.5 copy.1419
  1971.3 17.6 reduce-scatter.18.cloned.1.call-done
  1990.3 130.7 %reduce-scatter.20.cloned.1.call-done = f32[16,5]{1,0:T(8,128)} async-done(((f32[512,5]{1,0:T(8,128)}), f32[16,5]{1,0:T(8,128)}) %reduce-scatter.20.cloned.1.call-update) | async-done | bytes 336
  2122.4 130.4 %reduce-scatter.16.cloned.1.call-done = f32[16,227]{1,0:T(8,128)} async-done(((f32[512,227]{1,0:T(8,128)}), f32[16,227]{1,0:T(8,128)}) %reduce-scatter.16.cloned.1.call-update) | async-done | bytes 14544
  2254.3 354.0 %reduce-scatter.12.cloned.1.call-done = f32[12,16,512]{2,0,1:T(8,128)} async-done(((f32[12,512,512]{2,0,1:T(8,128)}), f32[12,16,512]{2,0,1:T(8,128)}) %reduce-scatter.12.cloned.1.call-update) | async-done | bytes 393232 | tf_op jit(solution)/shard_map/reduce_scatter | solution.py:76
  2613.3 40.5 %all-reduce = (f32[]{:T(128)}, f32[]{:T(128)}) all-reduce(f32[]{:T(128)S(6)} %add.749, f32[]{:T(128)S(6)} %add.775), channel_id=1, replica_groups=mesh['node'=16,'feat'=2] {'node','feat'}, use_global_device_ids=true, to_apply=%region_160.164 | all-reduce | flops 2 | bytes 16 | tf_op jit(solution)/shard_map/psum | solution.py:379
  (1711 shorter events, 1202.4 us)
Async XLA Ops:
  7.3 405.1 %all-gather.4.cloned.1.call-start = ((), (), s32[]{:S(2)}) async-start(), calls=%async_computation.53 | async-start | bytes 6488064 | tf_op jit(solution)/shard_map/all_gather | solution.py:66
  151.4 80.7 %all-to-all-start.28 = ((bf16[2,2,16384]{2,1,0:T(2,128)(2,1)}), bf16[2,2,16384]{2,1,0:T(2,128)(2,1)S(1)}, u32[]{:S(2)}, u32[]{:S(2)}) async-start(bf16[2,2,16384]{2,1,0:T(2,128)(2,1)} %reshape.1739), calls=%async_computation.28 | async-start | bytes 262144 | tf_op jit(solution)/shard_map/all_to_all | solution.py:49
  239.9 117.1 %all-to-all-start.14 = ((bf16[2,2,16384]{2,1,0:T(2,128)(2,1)}), bf16[2,2,16384]{2,1,0:T(2,128)(2,1)S(1)}, u32[]{:S(2)}, u32[]{:S(2)}) async-start(bf16[2,2,16384]{2,1,0:T(2,128)(2,1)} %reshape.1737), calls=%async_computation.14 | async-start | bytes 262144 | tf_op jit(solution)/shard_map/all_to_all | solution.py:49
  430.4 21.5 collective-permute-start
  444.7 72.2 %collective-permute-start.8 = (bf16[2,256,256]{2,1,0:T(8,128)(2,1)}, bf16[2,256,256]{2,1,0:T(8,128)(2,1)}, u32[]{:S(2)}, u32[]{:S(2)}) collective-permute-start(bf16[2,256,256]{2,1,0:T(8,128)(2,1)} %bitcast.268), channel_id=1, source_target_pairs={{0,2},{2,4},{4,6},{6,8},{8,10},{10,12},{12,14},{14,16},{16,18},{18... | collective-permute-start | bytes 786440 | tf_op jit(solution)/shard_map/ppermute | solution.py:23
  451.5 66.4 %collective-permute-start.4 = (bf16[2,256,256]{2,1,0:T(8,128)(2,1)}, bf16[2,256,256]{2,1,0:T(8,128)(2,1)}, u32[]{:S(2)}, u32[]{:S(2)}) collective-permute-start(bf16[2,256,256]{2,1,0:T(8,128)(2,1)} %bitcast.165), channel_id=1, source_target_pairs={{0,2},{2,4},{4,6},{6,8},{8,10},{10,12},{12,14},{14,16},{16,18},{18... | collective-permute-start | bytes 786440 | tf_op jit(solution)/shard_map/ppermute | solution.py:23
  540.9 80.6 %collective-permute-start.1 = (bf16[2,256,256]{2,1,0:T(8,128)(2,1)}, bf16[2,256,256]{2,1,0:T(8,128)(2,1)}, u32[]{:S(2)}, u32[]{:S(2)}) collective-permute-start(bf16[2,256,256]{2,1,0:T(8,128)(2,1)} %bitcast.72), channel_id=1, source_target_pairs={{0,2},{2,4},{4,6},{6,8},{8,10},{10,12},{12,14},{14,16},{16,18},{18... | collective-permute-start | bytes 786440 | tf_op jit(solution)/shard_map/ppermute | solution.py:23
  694.0 24.0 all-to-all-start.31
  738.7 13.6 all-to-all-start.32
  766.5 36.5 %collective-permute-start.5 = (bf16[2,256,256]{2,1,0:T(8,128)(2,1)}, bf16[2,256,256]{2,1,0:T(8,128)(2,1)}, u32[]{:S(2)}, u32[]{:S(2)}) collective-permute-start(bf16[2,256,256]{2,1,0:T(8,128)(2,1)} %bitcast.183), channel_id=1, source_target_pairs={{0,2},{2,4},{4,6},{6,8},{8,10},{10,12},{12,14},{14,16},{16,18},{18... | collective-permute-start | bytes 786440 | tf_op jit(solution)/shard_map/ppermute | solution.py:23
  864.2 13.4 all-to-all-start.19
  886.1 12.1 all-to-all-start.6
  906.1 18.3 all-to-all-start.34
  1001.1 22.4 all-to-all-start.23
  1071.0 13.4 all-to-all-start.38
  1296.0 85.8 %collective-permute-start.10 = (bf16[2,256,256]{2,1,0:T(8,128)(2,1)}, bf16[2,256,256]{2,1,0:T(8,128)(2,1)}, u32[]{:S(2)}, u32[]{:S(2)}) collective-permute-start(bf16[2,256,256]{2,1,0:T(8,128)(2,1)} %pad_maximum_fusion.22), channel_id=1, source_target_pairs={{0,30},{2,0},{4,2},{6,4},{8,6},{10,8},{12,10},{14,12},{16,14},{18,... | collective-permute-start | bytes 786440 | tf_op jit(solution)/shard_map/ppermute | solution.py:23
  1337.1 51.5 %collective-permute-start.2 = (bf16[2,256,256]{2,1,0:T(8,128)(2,1)}, bf16[2,256,256]{2,1,0:T(8,128)(2,1)}, u32[]{:S(2)}, u32[]{:S(2)}) collective-permute-start(bf16[2,256,256]{2,1,0:T(8,128)(2,1)} %pad_maximum_fusion.10), channel_id=1, source_target_pairs={{0,30},{2,0},{4,2},{6,4},{8,6},{10,8},{12,10},{14,12},{16,14},{18,... | collective-permute-start | bytes 786440 | tf_op jit(solution)/shard_map/ppermute | solution.py:23
  1385.1 12.6 all-to-all-start.39
  1412.9 557.1 %reduce-scatter.14.cloned.1.call-start = ((), (), s32[]{:S(2)}) async-start(), calls=%async_computation.55 | async-start | bytes 270336 | tf_op jit(solution)/shard_map/reduce_scatter | solution.py:78
  1455.1 15.0 all-to-all-start.26
  1685.2 82.0 %collective-permute-start.7 = (bf16[2,256,256]{2,1,0:T(8,128)(2,1)}, bf16[2,256,256]{2,1,0:T(8,128)(2,1)}, u32[]{:S(2)}, u32[]{:S(2)}) collective-permute-start(bf16[2,256,256]{2,1,0:T(8,128)(2,1)} %pad_maximum_fusion.17), channel_id=1, source_target_pairs={{0,30},{2,0},{4,2},{6,4},{8,6},{10,8},{12,10},{14,12},{16,14},{18,... | collective-permute-start | bytes 786440 | tf_op jit(solution)/shard_map/ppermute | solution.py:23
  1726.6 46.6 %collective-permute-start.3 = (bf16[2,256,256]{2,1,0:T(8,128)(2,1)}, bf16[2,256,256]{2,1,0:T(8,128)(2,1)}, u32[]{:S(2)}, u32[]{:S(2)}) collective-permute-start(bf16[2,256,256]{2,1,0:T(8,128)(2,1)} %pad_maximum_fusion.11), channel_id=1, source_target_pairs={{0,30},{2,0},{4,2},{6,4},{8,6},{10,8},{12,10},{14,12},{16,14},{18,... | collective-permute-start | bytes 786440 | tf_op jit(solution)/shard_map/ppermute | solution.py:23
  1769.6 12.7 all-to-all-start.27
  1794.1 11.9 all-to-all-start.41
  1821.7 34.6 %all-to-all-start.44 = ((bf16[2,2,16384]{2,1,0:T(2,128)(2,1)}), bf16[2,2,16384]{2,1,0:T(2,128)(2,1)}, u32[]{:S(2)}, u32[]{:S(2)}) async-start(bf16[2,2,16384]{2,1,0:T(2,128)(2,1)} %reshape.1801), calls=%async_computation.44 | async-start | bytes 262144 | tf_op jit(solution)/shard_map/all_to_all | solution.py:49
  1825.8 163.2 %reduce-scatter.18.cloned.1.call-start = ((), (), s32[]{:S(2)}) async-start(), calls=%async_computation.57 | async-start | bytes 270336
  1856.2 16.6 all-to-all-start.42
  1872.9 17.9 all-to-all-start.46
  1890.8 20.2 all-to-all-start.45
  1922.5 198.5 %reduce-scatter.20.cloned.1.call-start = ((), (), s32[]{:S(2)}) async-start(), calls=%async_computation.58 | async-start | bytes 270336
  1928.9 323.9 %reduce-scatter.16.cloned.1.call-start = ((), (), s32[]{:S(2)}) async-start(), calls=%async_computation.56 | async-start | bytes 540672
  1930.4 677.9 %reduce-scatter.12.cloned.1.call-start = ((), (), s32[]{:S(2)}) async-start(), calls=%async_computation.54 | async-start | bytes 17301504 | tf_op jit(solution)/shard_map/reduce_scatter | solution.py:76
  (421 other events, 19491.2 us)
Sparse Core Ops, SparseCore 0:
  11.7 73.4 all-gather.3
  1416.0 131.2 reduce-scatter.13
  1856.3 132.5 reduce-scatter.17
  1991.6 129.3 reduce-scatter.19
  2123.2 129.5 reduce-scatter.15
  2255.0 353.2 reduce-scatter.11
where the time goes:
time: 2690 us; the launch traced here: 2670 us
  waiting for transfers between devices  730 us (27%)
  other arithmetic  664 us (25%)
  local copies, waits for them, and re-layouts  605 us (22%)
  blocking collectives  350 us (13%)
  starting transfers between devices  179 us (7%)
  matrix products  110 us (4%)
  between operations  30.7 us (1%)
    reduce_scatter x1, waiting for transfers between devices, reduce_grads(): lax.psum_scatter(grad_mats, ('node', 'feat'), scatter_dimension=1, tiled=...  354 us
    unnamed x9, waiting for transfers between devices  279 us
    scatter-add x6, other arithmetic, attend_back(): jax.ops.segment_sum(grad_keys.reshape(-1, col_total), flat_ids, num_segme...  142 us
    scatter-add x6, other arithmetic, attend_back(): jax.ops.segment_sum(grad_values.reshape(-1, col_total), flat_ids, num_seg...  141 us
    gather x12, local copies, waits for them, and re-layouts, gather_edges(): jnp.take(keys_all, senders, axis=0)  118 us
    gather x12, local copies, waits for them, and re-layouts, gather_edges(): jnp.take(values_all, senders, axis=0)  115 us
    unnamed x60, other arithmetic  86.6 us
    unnamed x906, local copies, waits for them, and re-layouts  86.5 us
  transfers between devices with their start and end apart: 66, of which 33 were waited for; matrix products, arithmetic and copies ran while one was open for 36% of the time, Pallas kernels for 0%

commit v1 on v0

v1 whole, which is shorter than its diff:
```python
import functools

import jax
import jax.numpy as jnp
from jax import lax
from jax.experimental import pallas as pl
from jax.experimental.pallas import tpu as pltpu
from jax.sharding import PartitionSpec as P

HEADS = 8
STEP = 5
NORM_EPS = 1e-05
CLIP = 0.05
RATE = 0.02
BETA_ONE = 0.5
BETA_TWO = 0.5
DECAY = 0.01
ADAM_EPS = 1e-08
DEAD = -1e30
MESH = pl.DeviceIdType.MESH
F32 = jnp.float32
BF16 = jnp.bfloat16


def nn(left, right):
    return jnp.dot(left, right, preferred_element_type=F32)


def nt(left, right):
    return lax.dot_general(left, right, (((1,), (1,)), ((), ())), preferred_element_type=F32)


def tn(left, right):
    return lax.dot_general(left, right, (((0,), (0,)), ((), ())), preferred_element_type=F32)


def norm_parts(state):
    centre = state - jnp.mean(state, axis=-1, keepdims=True)
    spread = jnp.mean(centre * centre, axis=-1, keepdims=True)
    scale = lax.rsqrt(spread + NORM_EPS)
    return centre * scale, scale


def norm_back(grad, hat, scale, gain):
    inner = grad * gain
    mean_inner = jnp.mean(inner, axis=-1, keepdims=True)
    mean_hat = jnp.mean(inner * hat, axis=-1, keepdims=True)
    return scale * (inner - mean_inner - hat * mean_hat)


def column_sum(value):
    return jnp.sum(value, axis=0, keepdims=True)


def sigmoid(value):
    return 1.0 / (1.0 + jnp.exp(-value))


def silu_slope(value):
    gate = sigmoid(value)
    return gate * (1.0 + value * (1.0 - gate))


class Sizes:
    def __init__(self, node, feat, batches, half, width, layers, heads, slots, c_in, c_out):
        self.node, self.feat = node, feat
        self.batches, self.half, self.width = batches, half, width
        self.rows = 2 * half
        self.layers, self.heads, self.slots = layers, heads, slots
        self.c_in, self.c_out = c_in, c_out
        self.shard = width // (node * feat)
        self.depth = node // 4
        self.mats = 6 * layers + 1
        self.cols = width // feat
        self.near = heads // feat
        self.fused = self.shard % 16 == 0 and node % 4 == 0
        groups = [(0, 4)]
        for first in range(4, self.mats, 3):
            groups.append((first, 3))
        self.groups = groups


def step_kernel(sz, *refs):
    refs = list(refs)

    def take(count):
        out = refs[:count]
        del refs[:count]
        return out

    grid_ref, target_ref, area_ref, count_ref, g2m_ref, m2g_ref, send_ref, edge_ref = take(8)
    if sz.fused:
        mat_ref, in_ref, out_ref, gain_ref, bias_ref = take(5)
        share, scalars = take(2)
        full, total = take(2)
    else:
        full, weight_ref = take(2)
        total, scalars = take(2)
    (
        rows_in,
        aim,
        pre_enc,
        state,
        middle,
        pre_mlp,
        mixed,
        query,
        pair,
        prob,
        edge_bias,
        g_row,
        g_col,
        m_row,
        m_col,
        affine,
        affine_grad,
        final,
        grad_pred,
        low,
        pre_low,
        mid_low,
        n_one,
        n_two,
        hidden,
        d_own,
        d_far,
        pair_out,
        pair_in,
        loss_acc,
    ) = take(30)
    (s_rows, r_rows, s_aim, r_aim, s_kv, r_kv, s_mix, r_mix, s_pair, r_pair, s_far, r_far) = take(12)
    if sz.fused:
        got_c, got_x, got_z, got_y, tile, tile_far, tile_z = take(7)
        (gz_s, gz_r, g2_s, g2_r, g3_s, g3_r, g4_s, g4_r) = take(8)
        (rc_s, rc_r, rx_s, rx_r, rz_s, rz_r, ry_s, ry_r) = take(8)
        (t_s, t_r, tz_s, tz_r) = take(4)

    nb, rows, half, width, cols = sz.batches, sz.rows, sz.half, sz.width, sz.cols
    node = lax.axis_index("node")
    j = lax.axis_index("feat")
    other = 1 - j
    after = lax.rem(node + 1, sz.node)
    before = lax.rem(node + sz.node - 1, sz.node)
    partner = (node, other)
    mine = pl.ds(pl.multiple_of(j * cols, cols), cols)
    theirs = pl.ds(pl.multiple_of(other * cols, cols), cols)
    waits = []

    def remote(src, dst, s_sem, r_sem, device):
        return pltpu.make_async_remote_copy(
            src_ref=src, dst_ref=dst, send_sem=s_sem, recv_sem=r_sem, device_id=device, device_id_type=MESH
        )

    barrier = pltpu.get_barrier_semaphore()
    greet = [(after, j), (before, j), partner]
    if sz.fused:
        depth = sz.depth
        c = lax.rem(node, 2)
        x = lax.rem(node // 2, 2)
        z = node // 4

        def place(zz, xx, cc):
            return zz * 4 + xx * 2 + cc

        core_dev = (place(z, x, 1 - c), j)
        x_dev = (place(z, 1 - x, c), j)
        z_devs = [(place(lax.rem(z + step, depth), x, c), j) for step in range(1, depth)]
        greet = greet + [core_dev, x_dev] + z_devs
    for device in greet:
        pl.semaphore_signal(barrier, inc=1, device_id=device, device_id_type=MESH)
    pl.semaphore_wait(barrier, len(greet))

    lanes_c = lax.broadcasted_iota(jnp.int32, (1, cols), 1) // (width // sz.heads)
    mask_low = [(lanes_c == head).astype(F32).astype(BF16) for head in range(sz.near)]
    mask_full = [(lanes_c == head).astype(F32) for head in range(sz.near)]

    def w_full(index):
        return full[index].reshape(width, width)

    def w_cols(index, which):
        if sz.fused:
            return full[index, :, :, :, :, :, which].reshape(width, cols)
        return full[index, :, :, which].reshape(width, cols)

    def w_rows(index, which):
        if sz.fused:
            count = sz.depth // 2
            return full[index, pl.ds(which * count, count)].reshape(width // 2, width)
        return full[index, which]

    def put_total(index, value):
        total[index] = value.reshape(total.shape[1:])

    if sz.fused:
        n_groups = len(sz.groups)
        packed = jnp.concatenate(
            [
                in_ref[...],
                jnp.zeros((sz.shard, 256 - sz.c_in), F32),
                jnp.zeros((sz.shard, 128), F32),
                out_ref[...],
                jnp.zeros((sz.shard, 128 - sz.c_out), F32),
            ],
            axis=1,
        )
        small = jnp.concatenate(
            [
                gain_ref[...],
                jnp.zeros((3, sz.shard), F32),
                bias_ref[...],
                jnp.zeros((3, sz.shard), F32),
            ],
            axis=0,
        )
        small = jnp.concatenate([small, jnp.zeros((16, 128 - sz.shard), F32)], axis=1)
        small = jnp.concatenate([small, jnp.zeros((112, 128), F32)], axis=0)
        small = jnp.transpose(small)[0 : sz.shard, :]
        full[0, z, x, c, j] = jnp.concatenate([packed[:, 0:256], small, packed[:, 384:512]], axis=1).astype(BF16)
        for index in range(sz.mats - 1):
            full[1 + index, z, x, c, j] = mat_ref[index].astype(BF16)
        for g, (first, count) in enumerate(sz.groups):
            span = pl.ds(first, count)
            own = full.at[span, z, x, c, j]
            for step in range(1, depth):
                copy = remote(own, own, gz_s.at[g, step - 1], gz_r.at[g, step - 1], z_devs[step - 1])
                copy.start()
                waits.append(copy)

    for b in range(nb):
        block = jnp.concatenate(
            [grid_ref[b].astype(F32), jnp.zeros((256 - sz.c_in, half), F32)], axis=0
        )
        rows_in[b, j] = jnp.transpose(block).astype(BF16)
    cell = lax.broadcasted_iota(jnp.int32, (1, half), 1)
    for b in range(nb):
        weight = jnp.where(cell < count_ref[b : b + 1, 0:1], area_ref[...], 0.0)
        block = jnp.concatenate(
            [
                target_ref[b].astype(F32),
                jnp.zeros((127 - sz.c_out, half), F32),
                weight,
            ],
            axis=0,
        )
        aim[b, j] = jnp.transpose(block)
    copy_rows = remote(rows_in.at[:, j], rows_in.at[:, j], s_rows, r_rows, partner)
    copy_aim = remote(aim.at[:, j], aim.at[:, j], s_aim, r_aim, partner)
    copy_rows.start()
    copy_aim.start()
    waits += [copy_rows, copy_aim]

    if sz.fused:
        weight_sum = jnp.zeros((1, 1), F32)
        for b in range(nb):
            weight = jnp.where(cell < count_ref[b : b + 1, 0:1], area_ref[...], 0.0)
            weight_sum = weight_sum + jnp.sum(weight, axis=1, keepdims=True)
        tile[0, 0] = jnp.broadcast_to(weight_sum * float(sz.c_out), (8, 128))

        def tile_reduce(slot):
            for level, device in enumerate((core_dev, x_dev, partner)):
                copy = remote(
                    tile.at[slot, level], tile_far.at[slot, level], t_s.at[slot, level], t_r.at[slot, level], device
                )
                copy.start()
                copy.wait()
                tile[slot, level + 1] = tile[slot, level] + tile_far[slot, level]
            tile_z[slot, z] = tile[slot, 3]
            copies = []
            for step in range(1, depth):
                copy = remote(
                    tile.at[slot, 3], tile_z.at[slot, z], tz_s.at[slot, step - 1], tz_r.at[slot, step - 1], z_devs[step - 1]
                )
                copy.start()
                copies.append(copy)
            for step in range(1, depth):
                copies[step - 1].wait_send()
                source = lax.rem(z + depth - step, depth)
                remote(
                    tile.at[slot, 3], tile_z.at[slot, source], tz_s.at[slot, step - 1], tz_r.at[slot, step - 1], z_devs[step - 1]
                ).wait_recv()
            result = tile_z[slot, 0]
            for index in range(1, depth):
                result = result + tile_z[slot, index]
            return result

    def counts(ref, slots, height, live=None):
        wide = lax.broadcasted_iota(jnp.int32, (height, rows), 0)
        acc = jnp.zeros((height, rows), F32)
        for slot in range(slots):
            hit = wide == ref[slot : slot + 1, :]
            if live is not None:
                hit = jnp.logical_and(hit, live > slot)
            acc = acc + jnp.where(hit, 1.0, 0.0)
        return acc

    receiver = lax.broadcasted_iota(jnp.int32, (1, rows), 1)
    live = jnp.where(receiver < rows // 2, edge_ref[0:1, 0:1], edge_ref[0:1, 1:2])
    for part in range(2):
        wide = lax.broadcasted_iota(jnp.int32, (rows, rows), 0) + part * rows
        acc = jnp.zeros((rows, rows), F32)
        for slot in range(sz.slots):
            hit = jnp.logical_and(wide == send_ref[slot : slot + 1, :], live > slot)
            acc = acc + jnp.where(hit, 1.0, 0.0)
        acc = jnp.transpose(acc)
        edge_bias[:, part * rows : (part + 1) * rows] = jnp.where(acc > 0.5, jnp.log(jnp.maximum(acc, 1.0)), DEAD)
    k_g = g2m_ref.shape[0]
    k_m = m2g_ref.shape[0]
    table = counts(g2m_ref, k_g, rows)
    g_col[...] = table.astype(BF16)
    g_row[...] = jnp.transpose(table).astype(BF16)
    table = counts(m2g_ref, k_m, rows)
    m_col[...] = table.astype(BF16)
    m_row[...] = jnp.transpose(table).astype(BF16)
    affine_grad[...] = jnp.zeros_like(affine_grad)
    loss_acc[...] = jnp.zeros_like(loss_acc)

    if sz.fused:
        side_a = pl.ds(0, width // 2)
        side_b = pl.ds(width // 2, width // 2)

        def gather_two(g):
            first, count = sz.groups[g]
            span = pl.ds(first, count)
            for step in range(1, depth):
                there = full.at[span, lax.rem(z + depth - step, depth), x, c, j]
                remote(there, there, gz_s.at[g, step - 1], gz_r.at[g, step - 1], z_devs[step - 1]).wait_recv()
            part = full.at[span, :, x, c, j, :, side_a]
            copy = remote(part, part, g2_s.at[g, 0], g2_r.at[g, 0], x_dev)
            copy.start()
            waits.append(copy)
            part = full.at[span, :, x, c, j, :, side_b]
            copy = remote(part, part, g2_s.at[g, 1], g2_r.at[g, 1], partner)
            copy.start()
            waits.append(copy)

        def gather_three(g):
            first, count = sz.groups[g]
            span = pl.ds(first, count)
            part = full.at[span, :, 1 - x, c, j, :, side_a]
            remote(part, part, g2_s.at[g, 0], g2_r.at[g, 0], x_dev).wait_recv()
            part = full.at[span, :, :, c, j, :, side_a]
            copy = remote(part, part, g3_s.at[g, 0], g3_r.at[g, 0], partner)
            copy.start()
            waits.append(copy)
            part = full.at[span, :, x, c, other, :, side_b]
            remote(part, part, g2_s.at[g, 1], g2_r.at[g, 1], partner).wait_recv()
            part = full.at[span, :, x, c, :, :, side_b]
            copy = remote(part, part, g3_s.at[g, 1], g3_r.at[g, 1], x_dev)
            copy.start()
            waits.append(copy)

        def gather_four(g):
            first, count = sz.groups[g]
            span = pl.ds(first, count)
            part = full.at[span, :, :, c, other, :, side_a]
            remote(part, part, g3_s.at[g, 0], g3_r.at[g, 0], partner).wait_recv()
            part = full.at[span, :, 1 - x, c, :, :, side_b]
            remote(part, part, g3_s.at[g, 1], g3_r.at[g, 1], x_dev).wait_recv()
            part = full.at[span, :, :, c]
            copy = remote(part, part, g4_s.at[g], g4_r.at[g], core_dev)
            copy.start()
            waits.append(copy)

        def gather_done(g):
            first, count = sz.groups[g]
            part = full.at[pl.ds(first, count), :, :, 1 - c]
            remote(part, part, g4_s.at[g], g4_r.at[g], core_dev).wait_recv()

        gather_two(0)
        weight_total = tile_reduce(0)
        gather_three(0)
        gather_two(1)
        gather_four(0)
        gather_three(1)
        gather_two(2)
        gather_done(0)
    else:
        weight_total = jnp.broadcast_to(weight_ref[...], (8, 128))
        n_groups = 0

        def gather_two(g):
            pass

        gather_three = gather_four = gather_done = gather_two
    scalars[1] = weight_total
    total_one = scalars[1, 0:1, 0:1]

    remote(rows_in.at[:, other], rows_in.at[:, other], s_rows, r_rows, partner).wait_recv()
    remote(aim.at[:, other], aim.at[:, other], s_aim, r_aim, partner).wait_recv()

    in_cols = pl.ds(0, 256)
    small_cols = pl.ds(256, 128)
    out_cols = pl.ds(384, 128)

    def aux(which, size):
        if sz.fused:
            return full[0, :, :, :, :, :, which].reshape(width, size)
        return full[0, :, :, which].reshape(width, size)

    affine[...] = jnp.transpose(aux(small_cols, 128).astype(F32))[0:16, :]

    def gain_row(index):
        return affine[pl.ds(index, 1), :]

    def bias_row(index):
        return affine[pl.ds(8 + index, 1), :]

    def add_affine(index, value):
        affine_grad[pl.ds(index, 1), :] = affine_grad[pl.ds(index, 1), :] + value

    def each(body):
        def wrapped(b, carry):
            body(b)
            return carry

        lax.fori_loop(0, nb, wrapped, 0)

    def encode(b):
        pre = nt(rows_in[b].reshape(rows, 256), aux(in_cols, 256)) + bias_row(0)
        pre_enc[b] = pre
        enc = (pre * sigmoid(pre)).astype(BF16)
        start = nn(g_row[...], enc) * (1.0 / k_g)
        state[0, b] = start.astype(BF16).astype(F32)

    each(encode)

    def kv_copy(layer, b):
        return remote(
            pair.at[layer, b, :, pl.ds(0, rows)],
            pair.at[layer, b, :, pl.ds(rows, rows)],
            s_kv.at[layer, b],
            r_kv.at[layer, b],
            (after, j),
        )

    def mix_copy(layer, b):
        return remote(
            mixed.at[layer, b, j], mixed.at[layer, b, j], s_mix.at[layer, b], r_mix.at[layer, b], partner
        )

    def mix_wait(layer, b):
        there = mixed.at[layer, b, other]
        remote(there, there, s_mix.at[layer, b], r_mix.at[layer, b], partner).wait_recv()

    scale = float(width // sz.heads) ** -0.5

    def forward_layer(layer):
        base = 1 + 6 * layer

        def project(b):
            hat, _ = norm_parts(state[layer, b])
            normed = (hat * gain_row(2 * layer)).astype(BF16)
            query[layer, b] = nn(normed, w_cols(base, mine)).astype(BF16)
            pair[layer, b, 0, 0:rows] = nn(normed, w_cols(base + 1, mine)).astype(BF16)
            pair[layer, b, 1, 0:rows] = nn(normed, w_cols(base + 2, mine)).astype(BF16)
            kv_copy(layer, b).start()

        def attend(b):
            kv_copy(layer, b).wait_recv()
            keys, values, queries = pair[layer, b, 0], pair[layer, b, 1], query[layer, b]
            out = jnp.zeros((rows, cols), F32)
            for head in range(sz.near):
                score = nt(queries * mask_low[head], keys) * scale + edge_bias[...]
                expo = jnp.exp(score - jnp.max(score, axis=-1, keepdims=True))
                weight = (expo * (1.0 / jnp.sum(expo, axis=-1, keepdims=True))).astype(BF16)
                prob[layer, b, head] = weight
                out = out + nn(weight, values) * mask_full[head]
            mixed[layer, b, j] = out.astype(BF16)
            mix_copy(layer, b).start()

        def mlp(b):
            mix_wait(layer, b)
            mid = (
                state[layer, b]
                + nn(mixed[layer, b, 0], w_rows(base + 3, 0))
                + nn(mixed[layer, b, 1], w_rows(base + 3, 1))
            )
            middle[layer, b] = mid
            hat, _ = norm_parts(mid)
            normed = (hat * gain_row(2 * layer + 1)).astype(BF16)
            pre = nn(normed, w_full(base + 4)) + bias_row(1 + 2 * layer)
            pre_mlp[layer, b] = pre
            act = (pre * sigmoid(pre)).astype(BF16)
            state[layer + 1, b] = mid + nn(act, w_full(base + 5)) + bias_row(2 + 2 * layer)

        each(project)
        if layer == 0:
            gather_four(1)
            gather_three(2)
            gather_two(3)
        each(attend)
        if layer == 0:
            gather_done(1)
            gather_four(2)
            gather_three(3)
        each(mlp)
        if layer == 0:
            gather_done(2)
            gather_four(3)
            gather_done(3)

    for layer in range(sz.layers):
        forward_layer(layer)

    last = sz.layers
    lane_out = lax.broadcasted_iota(jnp.int32, (1, 128), 1)
    row_index = lax.broadcasted_iota(jnp.int32, (rows, 1), 0)
    own_row = jnp.logical_and(row_index >= j * half, row_index < (j + 1) * half).astype(F32)
    real_lane = (lane_out < sz.c_out).astype(F32)

    def decode(b):
        gain = gain_row(2 * sz.layers)
        dec = (nn(m_row[...], state[last, b].astype(BF16)) * (1.0 / k_m)).astype(BF16).astype(F32)
        hat, inv = norm_parts(dec)
        normed = (hat * gain).astype(BF16)
        final[b] = normed
        weights = aux(out_cols, 128)
        goal = aim[b].reshape(rows, 128)
        error = (nn(normed, weights) - goal) * real_lane
        weight = goal[:, 127:128]
        loss_acc[...] = loss_acc[...] + jnp.sum(
            jnp.sum((weight * own_row) * error * error, axis=1, keepdims=True), axis=0, keepdims=True
        )
        pred_low = (2.0 * weight * error / total_one).astype(BF16)
        grad_pred[b] = pred_low
        back = nt(pred_low, weights)
        add_affine(2 * sz.layers, column_sum(back * hat))
        dec_low = norm_back(back, hat, inv, gain).astype(BF16)
        state[last, b] = (nn(m_col[...], dec_low) * (1.0 / k_m)).astype(BF16).astype(F32)

    each(decode)

    if sz.fused:

        def reduce_core(g):
            first, count = sz.groups[g]
            span = pl.ds(first, count)
            copy = remote(total.at[span, :, :, 1 - c], got_c.at[span], rc_s.at[g], rc_r.at[g], core_dev)
            copy.start()
            waits.append(copy)

        def reduce_x(g):
            first, count = sz.groups[g]
            span = pl.ds(first, count)
            remote(got_c.at[span], got_c.at[span], rc_s.at[g], rc_r.at[g], core_dev).wait_recv()
            for index in range(first, first + count):
                total[index, :, :, c] = total[index, :, :, c] + got_c[index]
            copy = remote(total.at[span, :, 1 - x, c], got_x.at[span], rx_s.at[g], rx_r.at[g], x_dev)
            copy.start()
            waits.append(copy)

        def reduce_z(g):
            first, count = sz.groups[g]
            span = pl.ds(first, count)
            remote(got_x.at[span], got_x.at[span], rx_s.at[g], rx_r.at[g], x_dev).wait_recv()
            for index in range(first, first + count):
                total[index, :, x, c] = total[index, :, x, c] + got_x[index]
            for step in range(1, depth):
                to = lax.rem(z + step, depth)
                copy = remote(
                    total.at[span, to, x, c],
                    got_z.at[step - 1, span],
                    rz_s.at[g, step - 1],
                    rz_r.at[g, step - 1],
                    z_devs[step - 1],
                )
                copy.start()
                waits.append(copy)

        def reduce_y(g):
            first, count = sz.groups[g]
            span = pl.ds(first, count)
            for step in range(1, depth):
                there = got_z.at[step - 1, span]
                remote(there, there, rz_s.at[g, step - 1], rz_r.at[g, step - 1], z_devs[step - 1]).wait_recv()
            for index in range(first, first + count):
                acc = total[index, z, x, c]
                for step in range(1, depth):
                    acc = acc + got_z[step - 1, index]
                total[index, z, x, c] = acc
            send = total.at[span, z, x, c, pl.ds(pl.multiple_of(other * sz.shard, sz.shard), sz.shard)]
            copy = remote(send, got_y.at[span], ry_s.at[g], ry_r.at[g], partner)
            copy.start()
            waits.append(copy)

        def reduce_done(g):
            first, count = sz.groups[g]
            span = pl.ds(first, count)
            remote(got_y.at[span], got_y.at[span], ry_s.at[g], ry_r.at[g], partner).wait_recv()
            keep = pl.ds(pl.multiple_of(j * sz.shard, sz.shard), sz.shard)
            for index in range(first, first + count):
                share[index, :, mine] = total[index, z, x, c, keep]
                share[index, :, theirs] = got_y[index]

    else:

        def reduce_core(g):
            pass

        reduce_x = reduce_z = reduce_y = reduce_done = reduce_core

    def pair_copy(layer, b):
        return remote(
            pair_out.at[b], pair_in.at[layer, b], s_pair.at[layer, b], r_pair.at[layer, b], (before, j)
        )

    def far_copy(layer, b):
        return remote(d_own.at[b], d_far.at[layer, b], s_far.at[layer, b], r_far.at[layer, b], partner)

    def backward_layer(layer):
        base = 1 + 6 * layer

        def mlp_and_attention(b):
            grad = state[last, b]
            grad_low = grad.astype(BF16)
            low[b] = grad_low
            add_affine(8 + 2 + 2 * layer, column_sum(grad))
            pre = pre_mlp[layer, b]
            hidden[b] = (pre * sigmoid(pre)).astype(BF16)
            back = (nt(grad_low, w_full(base + 5)) * silu_slope(pre)).astype(BF16)
            pre_low[b] = back
            add_affine(8 + 1 + 2 * layer, column_sum(back.astype(F32)))
            back = nt(back, w_full(base + 4))
            gain = gain_row(2 * layer + 1)
            hat, inv = norm_parts(middle[layer, b])
            n_two[b] = (hat * gain).astype(BF16)
            add_affine(2 * layer + 1, column_sum(back * hat))
            grad = grad + norm_back(back, hat, inv, gain)
            state[last, b] = grad
            grad_low = grad.astype(BF16)
            mid_low[b] = grad_low
            grad_out = nt(grad_low, w_rows(base + 3, j)).astype(BF16)
            keys, values, queries = pair[layer, b, 0], pair[layer, b, 1], query[layer, b]
            d_query = jnp.zeros((rows, cols), F32)
            d_keys = jnp.zeros((2 * rows, cols), F32)
            d_values = jnp.zeros((2 * rows, cols), F32)
            for head in range(sz.near):
                weight_low = prob[layer, b, head]
                out_head = grad_out * mask_low[head]
                weight = weight_low.astype(F32)
                part = weight * nt(out_head, values)
                score = (part - weight * jnp.sum(part, axis=-1, keepdims=True)).astype(BF16)
                d_query = d_query + nn(score, keys) * mask_full[head]
                d_keys = d_keys + tn(score, queries * mask_low[head])
                d_values = d_values + tn(weight_low, out_head)
            d_own[b, :, 0:cols] = (d_query * scale).astype(BF16)
            d_keys = d_keys * scale
            pair_out[b, 0] = d_keys[rows:].astype(BF16)
            pair_out[b, 1] = d_values[rows:].astype(BF16)
            pair_copy(layer, b).start()
            pre_mlp[layer, b, :, 0:cols] = d_keys[0:rows]
            pre_mlp[layer, b, :, cols : 2 * cols] = d_values[0:rows]

        each(mlp_and_attention)
        many = nb * rows
        put_total(base + 5, tn(hidden[...].reshape(many, width), low[:, :, mine].reshape(many, cols)))
        put_total(base + 4, tn(n_two[...].reshape(many, width), pre_low[:, :, mine].reshape(many, cols)))
        grad_mid = mid_low[:, :, mine].reshape(many, cols)
        put_total(
            base + 3,
            jnp.concatenate(
                [
                    tn(mixed[layer, :, 0].reshape(many, cols), grad_mid),
                    tn(mixed[layer, :, 1].reshape(many, cols), grad_mid),
                ],
                axis=0,
            ),
        )
        reduce_core(2 * layer + 1)

        def finish_pair(b):
            pair_copy(layer, b).wait()
            d_own[b, :, cols : 2 * cols] = (pre_mlp[layer, b, :, 0:cols] + pair_in[layer, b, 0].astype(F32)).astype(BF16)
            d_own[b, :, 2 * cols : 3 * cols] = (
                pre_mlp[layer, b, :, cols : 2 * cols] + pair_in[layer, b, 1].astype(F32)
            ).astype(BF16)
            far_copy(layer, b).start()
            hat, _ = norm_parts(state[layer, b])
            n_one[b] = (hat * gain_row(2 * layer)).astype(BF16)

        each(finish_pair)
        reduce_x(2 * layer + 1)
        if layer + 1 < sz.layers:
            reduce_y(2 * layer + 3)
            reduce_z(2 * layer + 2)
        outer = tn(n_one[...].reshape(many, width), d_own[...].reshape(many, 3 * cols))
        for which in range(3):
            put_total(base + which, outer[:, which * cols : (which + 1) * cols])
        if layer > 0:
            reduce_core(2 * layer)

        def join(b):
            far_copy(layer, b).wait()
            back = jnp.zeros((rows, width), F32)
            for which in range(3):
                part = pl.ds(which * cols, cols)
                back = back + nt(d_own[b, :, part], w_cols(base + which, mine))
                back = back + nt(d_far[layer, b, :, part], w_cols(base + which, theirs))
            gain = gain_row(2 * layer)
            hat, inv = norm_parts(state[layer, b])
            add_affine(2 * layer, column_sum(back * hat))
            state[last, b] = state[last, b] + norm_back(back, hat, inv, gain)

        each(join)
        reduce_z(2 * layer + 1)
        if layer > 0:
            reduce_x(2 * layer)

    for layer in reversed(range(sz.layers)):
        backward_layer(layer)

    def encode_back(b):
        back = nn(g_col[...], state[last, b].astype(BF16)) * (1.0 / k_g)
        back = (back.astype(BF16).astype(F32) * silu_slope(pre_enc[b])).astype(BF16)
        pre_low[b] = back
        add_affine(8, column_sum(back.astype(F32)))

    each(encode_back)
    many = nb * rows
    wide = jnp.concatenate([affine_grad[...], jnp.zeros((112, width), F32)], axis=0)

    @pl.when(j == 0)
    def _():
        put_total(0, tn(pre_low[...].reshape(many, width), rows_in[...].reshape(many, 256)))

    @pl.when(j == 1)
    def _():
        put_total(
            0,
            jnp.concatenate(
                [
                    jnp.transpose(wide),
                    tn(final[...].reshape(many, width), grad_pred[...].reshape(many, 128)),
                ],
                axis=1,
            ),
        )

    if sz.fused:
        reduce_core(0)
        if sz.layers > 1:
            reduce_y(2)
        reduce_x(0)
        reduce_y(1)
        reduce_z(0)
        for g in range(1, n_groups):
            reduce_done(g)
        reduce_y(0)
        reduce_done(0)
        squares = jnp.zeros((1, 1), F32)
        for index in range(sz.mats):
            value = share[index]
            squares = squares + jnp.sum(
                jnp.sum(value * value, axis=1, keepdims=True), axis=0, keepdims=True
            )
        sub = lax.broadcasted_iota(jnp.int32, (8, 128), 0)
        tile[1, 0] = jnp.where(sub == 0, squares, loss_acc[0:1, 0:1])
        result = tile_reduce(1)
        scalars[0] = jnp.broadcast_to(result[1:2, :], (8, 128))
        scalars[2] = jnp.broadcast_to(jnp.sqrt(result[0:1, :]), (8, 128))
    else:
        scalars[0] = loss_acc[...]
        scalars[2] = loss_acc[...]

    for copy in waits:
        copy.wait_send()
    for layer in range(sz.layers):
        for b in range(nb):
            kv_copy(layer, b).wait_send()
            mix_copy(layer, b).wait_send()


def dma(*shape):
    return pltpu.SemaphoreType.DMA(shape)


def train_kernel(sz, operands):
    nb, rows, half, width, cols = sz.batches, sz.rows, sz.half, sz.width, sz.cols
    layers = sz.layers
    scratch = []
    if sz.fused:
        out_shape = (
            jax.ShapeDtypeStruct((sz.mats, sz.shard, width), F32),
            jax.ShapeDtypeStruct((3, 8, 128), F32),
        )
        scratch += [
            pltpu.VMEM((sz.mats, sz.depth, 2, 2, 2, sz.shard, width), BF16),
            pltpu.VMEM((sz.mats, sz.depth, 2, 2, 2 * sz.shard, cols), F32),
        ]
    else:
        out_shape = (
            jax.ShapeDtypeStruct((sz.mats, width, cols), F32),
            jax.ShapeDtypeStruct((3, 8, 128), F32),
        )
    scratch += [
        pltpu.VMEM((nb, 2, half, 256), BF16),
        pltpu.VMEM((nb, 2, half, 128), F32),
        pltpu.VMEM((nb, rows, width), F32),
        pltpu.VMEM((layers + 1, nb, rows, width), F32),
        pltpu.VMEM((layers, nb, rows, width), F32),
        pltpu.VMEM((layers, nb, rows, width), F32),
        pltpu.VMEM((layers, nb, 2, rows, cols), BF16),
        pltpu.VMEM((layers, nb, rows, cols), BF16),
        pltpu.VMEM((layers, nb, 2, 2 * rows, cols), BF16),
        pltpu.VMEM((layers, nb, sz.near, rows, 2 * rows), BF16),
        pltpu.VMEM((rows, 2 * rows), F32),
        pltpu.VMEM((rows, rows), BF16),
        pltpu.VMEM((rows, rows), BF16),
        pltpu.VMEM((rows, rows), BF16),
        pltpu.VMEM((rows, rows), BF16),
        pltpu.VMEM((16, width), F32),
        pltpu.VMEM((16, width), F32),
        pltpu.VMEM((nb, rows, width), BF16),
        pltpu.VMEM((nb, rows, 128), BF16),
        pltpu.VMEM((nb, rows, width), BF16),
        pltpu.VMEM((nb, rows, width), BF16),
        pltpu.VMEM((nb, rows, width), BF16),
        pltpu.VMEM((nb, rows, width), BF16),
        pltpu.VMEM((nb, rows, width), BF16),
        pltpu.VMEM((nb, rows, width), BF16),
        pltpu.VMEM((nb, rows, 3 * cols), BF16),
        pltpu.VMEM((layers, nb, rows, 3 * cols), BF16),
        pltpu.VMEM((nb, 2, rows, cols), BF16),
        pltpu.VMEM((layers, nb, 2, rows, cols), BF16),
        pltpu.VMEM((8, 128), F32),
    ]
    one = pltpu.SemaphoreType.DMA
    scratch += [one, one, one, one] + [dma(layers, nb)] * 8
    if sz.fused:
        depth, groups = sz.depth, len(sz.groups)
        scratch += [
            pltpu.VMEM((sz.mats, depth, 2, 2 * sz.shard, cols), F32),
            pltpu.VMEM((sz.mats, depth, 2 * sz.shard, cols), F32),
            pltpu.VMEM((depth - 1, sz.mats, 2 * sz.shard, cols), F32),
            pltpu.VMEM((sz.mats, sz.shard, cols), F32),
            pltpu.VMEM((2, 4, 8, 128), F32),
            pltpu.VMEM((2, 3, 8, 128), F32),
            pltpu.VMEM((2, depth, 8, 128), F32),
        ]
        far = [dma(groups, depth - 1)] * 2
        two = [dma(groups, 2)] * 4
        scratch += far + two + [dma(groups)] * 2
        scratch += [dma(groups)] * 4 + far + [dma(groups)] * 2
        scratch += [dma(2, 3)] * 2 + [dma(2, depth - 1)] * 2
    return pl.pallas_call(
        functools.partial(step_kernel, sz),
        out_shape=out_shape,
        in_specs=[pl.BlockSpec(memory_space=pltpu.VMEM)] * len(operands),
        out_specs=(pl.BlockSpec(memory_space=pltpu.VMEM),) * 2,
        scratch_shapes=scratch,
        compiler_params=pltpu.CompilerParams(
            collective_id=0, has_side_effects=True, vmem_limit_bytes=60 * 1024 * 1024
        ),
    )(*operands)


def adam(weight, first, second, grad):
    first_new = BETA_ONE * first + (1.0 - BETA_ONE) * grad
    second_new = BETA_TWO * second + (1.0 - BETA_TWO) * grad * grad
    first_hat = first_new / (1.0 - BETA_ONE**STEP)
    second_hat = second_new / (1.0 - BETA_TWO**STEP)
    weight_new = weight - RATE * (first_hat / (jnp.sqrt(second_hat) + ADAM_EPS) + DECAY * weight)
    return (weight_new, first_new, second_new, weight_new.astype(BF16))


def adam_kernel(sz, share, scalars, *refs):
    masters = refs[:15]
    outs = refs[15:35]
    mat, inp, out, gain, bias = [masters[3 * k : 3 * k + 3] for k in range(5)]
    factor = jnp.minimum(1.0, CLIP / (scalars[2, 0:1, 0:1] + 1e-06))

    def put(k, values):
        for ref, value in zip(outs[4 * k : 4 * k + 4], values):
            ref[...] = value

    for index in range(sz.mats - 1):
        values = adam(mat[0][index], mat[1][index], mat[2][index], factor * share[1 + index])
        for ref, value in zip(outs[0:4], values):
            ref[index] = value
    last = share[0]
    put(1, adam(inp[0][...], inp[1][...], inp[2][...], factor * last[:, 0 : sz.c_in]))
    put(2, adam(out[0][...], out[1][...], out[2][...], factor * last[:, 384 : 384 + sz.c_out]))
    small = jnp.concatenate([last[:, 256:384], jnp.zeros((128 - sz.shard, 128), F32)], axis=0)
    small = jnp.transpose(small)[:, 0 : sz.shard]
    count = gain[0].shape[0]
    put(3, adam(gain[0][...], gain[1][...], gain[2][...], factor * small[0:count]))
    put(4, adam(bias[0][...], bias[1][...], bias[2][...], factor * small[8 : 8 + count]))


def update(sz, share, scalars, groups):
    operands = [share, scalars]
    out_shape = []
    for triple in groups:
        operands += list(triple)
        shape = triple[0].shape
        out_shape += [jax.ShapeDtypeStruct(shape, F32)] * 3 + [jax.ShapeDtypeStruct(shape, BF16)]
    return pl.pallas_call(
        functools.partial(adam_kernel, sz),
        out_shape=tuple(out_shape),
        in_specs=[pl.BlockSpec(memory_space=pltpu.VMEM)] * len(operands),
        out_specs=(pl.BlockSpec(memory_space=pltpu.VMEM),) * len(out_shape),
    )(*operands)


def per_device(
    grid_in, targets, area, row_count, g2m, m2g, senders, edge_count,
    mat_w, mat_m, mat_v, in_w, in_m, in_v, out_w, out_m, out_v,
    gain_w, gain_m, gain_v, bias_w, bias_m, bias_v,
):
    axes = ("node", "feat")
    sz = Sizes(
        lax.axis_size("node"),
        lax.axis_size("feat"),
        grid_in.shape[0],
        grid_in.shape[1],
        mat_w.shape[2],
        mat_w.shape[0] // 6,
        HEADS,
        senders.shape[1],
        grid_in.shape[2],
        targets.shape[2],
    )
    operands = [
        jnp.swapaxes(grid_in, 1, 2),
        jnp.swapaxes(targets, 1, 2),
        area.reshape(1, -1),
        row_count,
        g2m.T,
        m2g.T,
        senders.T,
        edge_count.reshape(1, -1),
    ]
    if sz.fused:
        operands += [mat_w, in_w.T, out_w, gain_w, bias_w]
        share, scalars = train_kernel(sz, operands)
        groups = (
            (mat_w, mat_m, mat_v),
            (in_w.T, in_m.T, in_v.T),
            (out_w, out_m, out_v),
            (gain_w, gain_m, gain_v),
            (bias_w, bias_m, bias_v),
        )
        outs = list(update(sz, share, scalars, groups))
        for index in range(4, 8):
            outs[index] = outs[index].T
        return tuple(outs) + (scalars[0, 0, 0], scalars[1, 0, 0], scalars[2, 0, 0])

    width, shard = sz.width, sz.shard

    def pad(value, size):
        return jnp.pad(value, ((0, 0), (0, size - value.shape[1])))

    def pack(square, inp, out, gain, bias):
        small = jnp.concatenate([pad(gain.T, 8), pad(bias.T, 120)], axis=1)
        first = jnp.concatenate([pad(inp.T, 256), small, pad(out, 128)], axis=1)
        return jnp.concatenate([first[None], square], axis=0)

    packed = pack(mat_w, in_w, out_w, gain_w, bias_w).astype(BF16)
    full = lax.all_gather(packed, axes, axis=1, tiled=True).reshape(sz.mats, 2, width // 2, width)
    live = (jnp.arange(sz.half)[None, :] < row_count).astype(F32)
    weight_total = lax.psum(jnp.sum(area[None, :] * live) * targets.shape[2], axes)
    operands += [full, weight_total.reshape(1, 1)]
    part, scalars = train_kernel(sz, operands)
    feat = lax.axis_index("feat")
    spread = lax.dynamic_update_slice(
        jnp.zeros((sz.mats, width, width), F32), part, (0, 0, feat * sz.cols)
    )
    share = lax.psum_scatter(spread, axes, scatter_dimension=1, tiled=True)
    square_sum, loss_sum = lax.psum((jnp.sum(share * share), scalars[0, 0, 0]), axes)
    grad_norm = jnp.sqrt(square_sum)
    share = jnp.minimum(1.0, CLIP / (grad_norm + 1e-06)) * share
    count = gain_w.shape[0]
    last = share[0]
    outs = adam(mat_w, mat_m, mat_v, share[1:])
    outs += adam(in_w, in_m, in_v, last[:, 0 : sz.c_in].T)
    outs += adam(out_w, out_m, out_v, last[:, 384 : 384 + sz.c_out])
    outs += adam(gain_w, gain_m, gain_v, last[:, 256 : 256 + count].T)
    outs += adam(bias_w, bias_m, bias_v, last[:, 264 : 264 + count].T)
    return outs + (loss_sum, weight_total, grad_norm)


def solution(mesh):
    both = ("node", "feat")
    rows_three = P(None, both, None)
    second = P(None, both)
    first = P(both, None)
    placed = (
        rows_three, rows_three, P(both), second,
        P("node", None), P("node", None), P("node", None), P("node"),
    )
    placed += (rows_three,) * 3 + (second,) * 3 + (first,) * 3 + (second,) * 6
    outs = (rows_three,) * 4 + (second,) * 4 + (first,) * 4 + (second,) * 8 + (P(), P(), P())
    return jax.shard_map(per_device, mesh=mesh, in_specs=placed, out_specs=outs, check_vma=False)
```

time: 2690 us -> 216 us (0.08)
  waiting for transfers between devices: 730 us -> 0 us
  other arithmetic: 664 us -> 0 us
  local copies, waits for them, and re-layouts: 605 us -> 2.52 us
  blocking collectives: 350 us -> 0 us
  Pallas kernels: 0 us -> 213 us
  starting transfers between devices: 179 us -> 0 us
  matrix products: 110 us -> 0 us
  between operations: 30.7 us -> 0.68 us
    reduce_scatter x2 -> x0, waiting for transfers between devices: 354 us -> none  [the longest x1 354 us: reduce_grads(): lax.psum_scatter(grad_mats, ('node', 'feat'), scatter_dimension=1, tiled=...]
    scatter-add x18 -> x0, other arithmetic: 337 us -> none  [the longest x6 142 us: attend_back(): jax.ops.segment_sum(grad_keys.reshape(-1, col_total), flat_ids, num_segme...]
    unnamed x9 -> x0, waiting for transfers between devices: 279 us -> none
    all_gather x4 -> x0, blocking collectives: 273 us -> none  [the longest x1 71.6 us: fetch_all(): lax.all_gather(out_w.astype(jnp.bfloat16), ('node', 'feat'), axis=0, tile...]
    gather x33 -> x0, local copies, waits for them, and re-layouts: 265 us -> none  [the longest x12 118 us: gather_edges(): jnp.take(keys_all, senders, axis=0)]
    pallas_call x0 -> x2, Pallas kernels: none -> 213 us  [the longest x1 210 us: train_kernel(): pl.pallas_call(functools.partial(step_kernel, sz), out_shape=out_shape, i...]
    all_to_all x48 -> x0, starting transfers between devices: 171 us -> none  [the longest x24 85.4 us: to_columns(): lax.all_to_all(stacked, 'feat', split_axis=2, concat_axis=1, tiled=True)]
    dot_general x87 -> x0, matrix products: 110 us -> none  [the longest x24 29.2 us: product(): return jnp.dot(left, right, preferred_element_type=jnp.float32)]
  transfers between devices with their start and end apart: 66 -> 0, of which waited for: 33 -> 0; matrix products, arithmetic and copies ran while one was open for 36% -> 0% of each run, Pallas kernels for 0% -> 0%
where the time goes in v1:
time: 216 us
  Pallas kernels  213 us (99%)
  local copies, waits for them, and re-layouts  2.52 us (1%)
    pallas_call x1, Pallas kernels, train_kernel(): pl.pallas_call(functools.partial(step_kernel, sz), out_shape=out_shape, i...  210 us

profile of v1, /device:TPU:0, one launch (start us, length us, event | category | flops | bytes accessed | tf_op | source)
XLA Modules:
  0.0 216.2 jit_solution(7049211367289317134)
XLA Ops:
  0.7 0.0 copy-start
  0.7 0.6 copy-done
  1.3 0.7 copy.46.refs_3_
  2.0 210.1 %shard_map.398 = (f32[13,16,512]{2,1,0:T(8,128)}, f32[3,8,128]{2,1,0:T(8,128)}) custom-call(bf16[3,227,128]{2,1,0:T(8,128)(2,1)} %bitcast.17, bf16[3,83,128]{2,1,0:T(8,128)(2,1)} %bitcast.18, f32[1,128]{1,0:T(1,128)} %bitcast.26, s32[3,1]{1,0:T(4,128)} %copy.46.refs_3_, s32[8,256]{1,0:T(8,128)} %bitcast.24, s32[3,256]{1,0:T(4,128)} %bitcast.25, ...), custom_call_target="tpu_custom_call" | custom-call | tf_op jit(solution)/shard_map/pallas_call | solution.py:845
  212.0 2.9 %shard_map.399 = (f32[12,16,512]{2,1,0:T(8,128)}, f32[12,16,512]{2,1,0:T(8,128)}, f32[12,16,512]{2,1,0:T(8,128)}, bf16[12,16,512]{2,1,0:T(8,128)(2,1)}, f32[16,2...) custom-call(f32[13,16,512]{2,1,0:T(8,128)} %get-tuple-element.45.sha, ...), custom_call_target="tpu_custom_call" | custom-call | tf_op jit(solution)/shard_map/pallas_call | solution.py:897
  215.0 1.2 fusion
Async XLA Ops:
  0.7 0.7 copy-start

commit v2 on v1

v2 whole, which is shorter than its diff:
```python
import functools

import jax
import jax.numpy as jnp
from jax import lax
from jax.experimental import pallas as pl
from jax.experimental.pallas import tpu as pltpu
from jax.sharding import PartitionSpec as P

HEADS = 8
STEP = 5
NORM_EPS = 1e-05
CLIP = 0.05
RATE = 0.02
BETA_ONE = 0.5
BETA_TWO = 0.5
DECAY = 0.01
ADAM_EPS = 1e-08
DEAD = -1e30
MESH = pl.DeviceIdType.MESH
F32 = jnp.float32
BF16 = jnp.bfloat16


def nn(left, right):
    return jnp.dot(left, right, preferred_element_type=F32)


def nt(left, right):
    return lax.dot_general(left, right, (((1,), (1,)), ((), ())), preferred_element_type=F32)


def tn(left, right):
    return lax.dot_general(left, right, (((0,), (0,)), ((), ())), preferred_element_type=F32)


def norm_parts(state):
    centre = state - jnp.mean(state, axis=-1, keepdims=True)
    spread = jnp.mean(centre * centre, axis=-1, keepdims=True)
    scale = lax.rsqrt(spread + NORM_EPS)
    return centre * scale, scale


def norm_back(grad, hat, scale, gain):
    inner = grad * gain
    mean_inner = jnp.mean(inner, axis=-1, keepdims=True)
    mean_hat = jnp.mean(inner * hat, axis=-1, keepdims=True)
    return scale * (inner - mean_inner - hat * mean_hat)


def column_sum(value):
    return jnp.sum(value, axis=0, keepdims=True)


def sigmoid(value):
    return 1.0 / (1.0 + jnp.exp(-value))


def silu_slope(value):
    gate = sigmoid(value)
    return gate * (1.0 + value * (1.0 - gate))


class Sizes:
    def __init__(self, node, feat, batches, half, width, layers, heads, slots, c_in, c_out):
        self.node, self.feat = node, feat
        self.batches, self.half, self.width = batches, half, width
        self.rows = 2 * half
        self.layers, self.heads, self.slots = layers, heads, slots
        self.c_in, self.c_out = c_in, c_out
        self.shard = width // (node * feat)
        self.depth = node // 4
        self.mats = 6 * layers + 1
        self.cols = width // feat
        self.near = heads // feat
        self.fused = self.shard % 16 == 0 and node % 4 == 0
        self.groups = [(0, 1)] + [(first, 3) for first in range(1, self.mats, 3)]
        self.units = [(0, 1)]
        for layer in range(layers):
            self.units += [(1 + 6 * layer, 4), (5 + 6 * layer, 2)]


def step_kernel(sz, *refs):
    refs = list(refs)

    def take(count):
        out = refs[:count]
        del refs[:count]
        return out

    grid_ref, target_ref, area_ref, count_ref, g2m_ref, m2g_ref, send_ref, edge_ref = take(8)
    if sz.fused:
        mat_ref, in_ref, out_ref, gain_ref, bias_ref = take(5)
        share, scalars = take(2)
        full, total = take(2)
    else:
        full, weight_ref = take(2)
        total, scalars = take(2)
    (
        rows_own,
        rows_in,
        rows_prev,
        indices,
        start,
        start_prev,
        state,
        middle,
        pre_mlp,
        mixed,
        query,
        pair,
        prob,
        edge_bias,
        g_row,
        g_col,
        gp_row,
        gp_col,
        m_row,
        m_col,
        affine,
        affine_grad,
        final,
        grad_pred,
        low,
        pre_low,
        mid_low,
        n_own,
        n_prev,
        n_two,
        hidden,
        d_own,
        d_far,
        dn_out,
        dn_in,
        loss_acc,
    ) = take(36)
    (s_rows, r_rows, s_idx, r_idx, s_prev, r_prev) = take(6)
    (s_n, r_n, s_nf, r_nf, s_mix, r_mix, s_dn, r_dn, s_df, r_df, s_far, r_far) = take(12)
    (far_free,) = take(1)
    if sz.fused:
        (code_one, got_one, code_two, got_two, code_z, got_z, got_c) = take(7)
        (size_out, size_in, size_z, size_z_in, tile, tile_far, tile_all) = take(7)
        (gz_s, gz_r, g2_s, g2_r, g3_s, g3_r, g4_s, g4_r) = take(8)
        (rr_s, rr_r, rz_s, rz_r, rc_s, rc_r) = take(6)
        (t_s, t_r, tz_s, tz_r) = take(4)

    nb, rows, half, width, cols = sz.batches, sz.rows, sz.half, sz.width, sz.cols
    node = lax.axis_index("node")
    y = lax.axis_index("feat")
    waits = []
    if sz.fused:
        depth = sz.depth
        c = lax.rem(node, 2)
        x = lax.rem(node // 2, 2)
        z = node // 4
        j = c

        def device_of(zz, xx, cc, yy):
            return (zz * 4 + xx * 2 + cc, yy)

        def holder(block):
            return device_of(block // 4, lax.rem(block // 2, 2), c, lax.rem(block, 2))

        block = z * 4 + x * 2 + y
        after = holder(lax.rem(block + 1, sz.node))
        before = holder(lax.rem(block + sz.node - 1, sz.node))
        partner = device_of(z, x, 1 - c, y)
        x_dev = device_of(z, 1 - x, c, y)
        y_dev = device_of(z, x, c, 1 - y)
        z_devs = [device_of(lax.rem(z + step, depth), x, c, y) for step in range(1, depth)]

        def chip_at(dz, dx, dy):
            return device_of(lax.rem(z + dz, depth), lax.rem(x + dx, 2), c, lax.rem(y + dy, 2))

        offsets = [(k // 4, (k // 2) % 2, k % 2) for k in range(1, 4 * depth)]
        greet = [after, before, partner] + [chip_at(*offset) for offset in offsets]
    else:
        j = y
        after = (lax.rem(node + 1, sz.node), j)
        before = (lax.rem(node + sz.node - 1, sz.node), j)
        partner = (node, 1 - j)
        greet = [after, before, partner]
    other = 1 - j
    mine = pl.ds(pl.multiple_of(j * cols, cols), cols)
    theirs = pl.ds(pl.multiple_of(other * cols, cols), cols)

    def remote(src, dst, s_sem, r_sem, device):
        return pltpu.make_async_remote_copy(
            src_ref=src, dst_ref=dst, send_sem=s_sem, recv_sem=r_sem, device_id=device, device_id_type=MESH
        )

    def push(make):
        make().start()
        waits.append(make)

    barrier = pltpu.get_barrier_semaphore()
    for device in greet:
        pl.semaphore_signal(barrier, inc=1, device_id=device, device_id_type=MESH)
    pl.semaphore_wait(barrier, len(greet))

    lanes_c = lax.broadcasted_iota(jnp.int32, (1, cols), 1) // (width // sz.heads)
    mask_low = [(lanes_c == head).astype(F32).astype(BF16) for head in range(sz.near)]
    mask_full = [(lanes_c == head).astype(F32) for head in range(sz.near)]

    def w_full(index):
        return full[index].reshape(width, width)

    def w_cols(index, which):
        if sz.fused:
            return full[index, :, :, :, :, :, which].reshape(width, cols)
        return full[index, :, :, which].reshape(width, cols)

    def w_rows(index, which):
        if sz.fused:
            count = sz.depth // 2
            return full[index, pl.ds(which * count, count)].reshape(width // 2, width)
        return full[index, which]

    def w_block(index, rows_half, which):
        if sz.fused:
            count = sz.depth // 2
            return full[index, pl.ds(rows_half * count, count), :, :, :, :, which].reshape(width // 2, cols)
        return full[index, rows_half, :, which]

    def put_total(index, value):
        total[index] = value.reshape(total.shape[1:])

    cell = lax.broadcasted_iota(jnp.int32, (1, half), 1)
    for b in range(nb):
        block_in = jnp.concatenate([grid_ref[b].astype(F32), jnp.zeros((256 - sz.c_in, half), F32)], axis=0)
        rows_own[b, :, 0:256] = jnp.transpose(block_in).astype(BF16)
        weight = jnp.where(cell < count_ref[b : b + 1, 0:1], area_ref[...], 0.0)
        first = weight.astype(BF16).astype(F32)
        second = (weight - first).astype(BF16).astype(F32)
        third = weight - first - second
        block_in = jnp.concatenate(
            [target_ref[b].astype(F32), jnp.zeros((125 - sz.c_out, half), F32), first, second, third], axis=0
        )
        rows_own[b, :, 256:384] = jnp.transpose(block_in).astype(BF16)
    slot = c if sz.fused else 0
    k_g = g2m_ref.shape[0]
    k_m = m2g_ref.shape[0]
    receiver = lax.broadcasted_iota(jnp.int32, (1, rows), 1)
    indices[slot, 0:k_g] = g2m_ref[...]
    indices[slot, 8 : 8 + k_m] = m2g_ref[...]
    indices[slot, 15:16] = jnp.where(receiver < rows // 2, edge_ref[0:1, 0:1], edge_ref[0:1, 1:2])
    indices[slot, 16 : 16 + sz.slots] = send_ref[...]
    here = rows_in.at[:, y]
    there = rows_in.at[:, 1 - y]
    if sz.fused:
        push(lambda: remote(indices.at[c], indices.at[c], s_idx.at[0], r_idx.at[0], partner))
        to_partner = remote(rows_own, here, s_rows.at[0], r_rows.at[0], partner)
        to_chip = remote(rows_own, here, s_rows.at[1], r_rows.at[1], y_dev)
        forward = remote(there, there, s_rows.at[2], r_rows.at[1], partner)

        @pl.when(c == y)
        def _():
            to_partner.start()
            rows_in[:, y] = rows_own[...]

        @pl.when(c != y)
        def _():
            to_chip.start()

    else:
        push(lambda: remote(rows_own, here, s_rows.at[0], r_rows.at[0], partner))
        rows_in[:, y] = rows_own[...]

    if sz.fused:
        n_groups = len(sz.groups)
        packed = jnp.concatenate(
            [
                in_ref[...],
                jnp.zeros((sz.shard, 256 - sz.c_in), F32),
                jnp.zeros((sz.shard, 128), F32),
                out_ref[...],
                jnp.zeros((sz.shard, 128 - sz.c_out), F32),
            ],
            axis=1,
        )
        small = jnp.concatenate(
            [
                gain_ref[...],
                jnp.zeros((3, sz.shard), F32),
                bias_ref[...],
                jnp.zeros((3, sz.shard), F32),
            ],
            axis=0,
        )
        small = jnp.concatenate([small, jnp.zeros((16, 128 - sz.shard), F32)], axis=1)
        small = jnp.concatenate([small, jnp.zeros((112, 128), F32)], axis=0)
        small = jnp.transpose(small)[0 : sz.shard, :]
        full[0, z, x, c, y] = jnp.concatenate([packed[:, 0:256], small, packed[:, 384:512]], axis=1).astype(BF16)
        for index in range(sz.mats - 1):
            full[1 + index, z, x, c, y] = mat_ref[index].astype(BF16)

        def gather_one(g):
            first, count = sz.groups[g]
            for step in range(1, depth):

                def make(g=g, first=first, count=count, step=step):
                    own = full.at[pl.ds(first, count), z, x, c, y]
                    return remote(own, own, gz_s.at[g, step - 1], gz_r.at[g, step - 1], z_devs[step - 1])

                push(make)

        gather_one(0)
        gather_one(1)
        gather_one(2)

    if sz.fused:
        weight_sum = jnp.zeros((1, 1), F32)
        for b in range(nb):
            weight = jnp.where(cell < count_ref[b : b + 1, 0:1], area_ref[...], 0.0)
            weight_sum = weight_sum + jnp.sum(weight, axis=1, keepdims=True)
        tile[0, 0] = jnp.broadcast_to(weight_sum * float(sz.c_out), (8, 128))

        def tile_core(slot):
            return remote(tile.at[slot, 0], tile_far.at[slot], t_s.at[slot], t_r.at[slot], partner)

        def tile_chip(slot, k, place):
            return remote(
                tile.at[slot, 1], tile_all.at[slot, place], tz_s.at[slot, k], tz_r.at[slot, k], chip_at(*offsets[k])
            )

        def tile_start(slot):
            tile_core(slot).start()
            tile_core(slot).wait()
            tile[slot, 1] = tile[slot, 0] + tile_far[slot]
            spot = z * 4 + x * 2 + y
            tile_all[slot, spot] = tile[slot, 1]
            for k in range(len(offsets)):
                tile_chip(slot, k, spot).start()

        def tile_end(slot):
            for k, (dz, dx, dy) in enumerate(offsets):
                source = (
                    lax.rem(z + depth - dz, depth) * 4 + lax.rem(x + 2 - dx, 2) * 2 + lax.rem(y + 2 - dy, 2)
                )
                tile_chip(slot, k, source).wait()
            result = tile_all[slot, 0]
            for index in range(1, 4 * depth):
                result = result + tile_all[slot, index]
            return result

        tile_start(0)

    if sz.fused:
        remote(indices.at[1 - c], indices.at[1 - c], s_idx.at[0], r_idx.at[0], partner).wait_recv()
        slot = y
    push(lambda: remote(indices.at[slot], indices.at[2], s_idx.at[1], r_idx.at[1], after))

    def counts(place, first, slots, origin, live=None):
        wide = lax.broadcasted_iota(jnp.int32, (rows, rows), 0) + origin
        acc = jnp.zeros((rows, rows), F32)
        for k in range(slots):
            hit = wide == indices[place, first + k : first + k + 1, :]
            if live is not None:
                hit = jnp.logical_and(hit, live > k)
            acc = acc + jnp.where(hit, 1.0, 0.0)
        return acc

    live = indices[slot, 15:16, :]
    for part in range(2):
        acc = jnp.transpose(counts(slot, 16, sz.slots, part * rows, live))
        edge_bias[:, part * rows : (part + 1) * rows] = jnp.where(acc > 0.5, jnp.log(jnp.maximum(acc, 1.0)), DEAD)
    table = counts(slot, 0, k_g, 0)
    g_col[...] = table.astype(BF16)
    g_row[...] = jnp.transpose(table).astype(BF16)
    table = counts(slot, 8, k_m, 0)
    m_col[...] = table.astype(BF16)
    m_row[...] = jnp.transpose(table).astype(BF16)
    affine_grad[...] = jnp.zeros_like(affine_grad)
    loss_acc[...] = jnp.zeros_like(loss_acc)

    if sz.fused:

        @pl.when(c == y)
        def _():
            remote(there, there, s_rows.at[1], r_rows.at[1], y_dev).wait_recv()
            forward.start()
            to_partner.wait_send()
            forward.wait_send()

        @pl.when(c != y)
        def _():
            to_chip.wait_send()
            remote(here, here, s_rows.at[0], r_rows.at[0], partner).wait_recv()
            remote(there, there, s_rows.at[2], r_rows.at[1], partner).wait_recv()

    else:
        remote(there, there, s_rows.at[0], r_rows.at[0], partner).wait_recv()

    push(lambda: remote(rows_in.at[:, j, :, 0:256], rows_prev.at[:, j], s_prev.at[0], r_prev.at[0], after))

    if sz.fused:
        side_a = pl.ds(0, width // 2)
        side_b = pl.ds(width // 2, width // 2)

        def gather_part(g, stage, which):
            span = pl.ds(*sz.groups[g])
            if stage == 2:
                return full.at[span, :, x, c, y, :, which]
            if which is side_a:
                return full.at[span, :, :, c, y, :, which]
            return full.at[span, :, x, c, :, :, which]

        def gather_push(g, stage, side, sems, device):
            which = (side_a, side_b)[side]

            def make():
                part = gather_part(g, stage, which)
                return remote(part, part, sems[0].at[g, side], sems[1].at[g, side], device)

            push(make)

        def arrived(part, s_sem, r_sem, device):
            remote(part, part, s_sem, r_sem, device).wait_recv()

        def gather_two(g):
            span = pl.ds(*sz.groups[g])
            for step in range(1, depth):
                there = full.at[span, lax.rem(z + depth - step, depth), x, c, y]
                arrived(there, gz_s.at[g, step - 1], gz_r.at[g, step - 1], z_devs[step - 1])
            gather_push(g, 2, 0, (g2_s, g2_r), x_dev)
            gather_push(g, 2, 1, (g2_s, g2_r), y_dev)

        def gather_three(g):
            span = pl.ds(*sz.groups[g])
            arrived(full.at[span, :, 1 - x, c, y, :, side_a], g2_s.at[g, 0], g2_r.at[g, 0], x_dev)
            gather_push(g, 3, 0, (g3_s, g3_r), y_dev)
            arrived(full.at[span, :, x, c, 1 - y, :, side_b], g2_s.at[g, 1], g2_r.at[g, 1], y_dev)
            gather_push(g, 3, 1, (g3_s, g3_r), x_dev)

        def gather_four(g):
            span = pl.ds(*sz.groups[g])
            arrived(full.at[span, :, :, c, 1 - y, :, side_a], g3_s.at[g, 0], g3_r.at[g, 0], y_dev)
            arrived(full.at[span, :, 1 - x, c, :, :, side_b], g3_s.at[g, 1], g3_r.at[g, 1], x_dev)

            def make():
                part = full.at[span, :, :, c]
                return remote(part, part, g4_s.at[g], g4_r.at[g], partner)

            push(make)

        def gather_done(g):
            span = pl.ds(*sz.groups[g])
            arrived(full.at[span, :, :, 1 - c], g4_s.at[g], g4_r.at[g], partner)

    def gathered(stage, g):
        if sz.fused and g < len(sz.groups):
            (None, gather_one, gather_two, gather_three, gather_four, gather_done)[stage](g)

    gathered(2, 0)
    gathered(1, 3)
    gathered(2, 1)
    gathered(1, 4)
    gathered(3, 0)
    for g in range(5, len(sz.groups)):
        gathered(1, g)

    in_cols = pl.ds(0, 256)
    small_cols = pl.ds(256, 128)
    out_cols = pl.ds(384, 128)

    def aux(which, size):
        if sz.fused:
            return full[0, :, :, :, :, :, which].reshape(width, size)
        return full[0, :, :, which].reshape(width, size)

    remote(indices.at[slot], indices.at[2], s_idx.at[1], r_idx.at[1], after).wait_recv()
    table = counts(2, 0, k_g, 0)
    gp_col[...] = table.astype(BF16)
    gp_row[...] = jnp.transpose(table).astype(BF16)
    remote(rows_prev.at[:, j], rows_prev.at[:, j], s_prev.at[0], r_prev.at[0], after).wait_recv()
    push(lambda: remote(rows_prev.at[:, j], rows_prev.at[:, j], s_prev.at[1], r_prev.at[1], partner))
    gathered(3, 1)
    gathered(2, 2)
    gathered(4, 0)
    gathered(4, 1)
    gathered(5, 0)
    remote(rows_prev.at[:, other], rows_prev.at[:, other], s_prev.at[1], r_prev.at[1], partner).wait_recv()

    affine[...] = jnp.transpose(aux(small_cols, 128).astype(F32))[0:16, :]

    def gain_row(index):
        return affine[pl.ds(index, 1), :]

    def bias_row(index):
        return affine[pl.ds(8 + index, 1), :]

    def add_affine(index, value):
        affine_grad[pl.ds(index, 1), :] = affine_grad[pl.ds(index, 1), :] + value

    def staggered(*bodies, hooks=()):
        def wrapped(t, carry):
            for step, hook in enumerate(hooks):
                if hook is not None:
                    pl.when(t == step)(hook)
            for late in reversed(range(len(bodies))):

                @pl.when(jnp.logical_and(t >= late, t < nb + late))
                def _(late=late):
                    bodies[late](t - late)

            return carry

        lax.fori_loop(0, nb + len(bodies) - 1, wrapped, 0)

    def each(body, hooks=()):
        def wrapped(b, carry):
            for step, hook in enumerate(hooks):
                if hook is not None:
                    pl.when(b == step)(hook)
            body(b)
            return carry

        lax.fori_loop(0, nb, wrapped, 0)

    def pre_encode(ref, b):
        return nt(ref[b, :, :, 0:256].reshape(rows, 256), aux(in_cols, 256)) + bias_row(0)

    def encode(b):
        gain = gain_row(0)
        for ref, table, keep, normed in (
            (rows_in, g_row, start, n_own),
            (rows_prev, gp_row, start_prev, n_prev),
        ):
            pre = pre_encode(ref, b)
            enc = (pre * sigmoid(pre)).astype(BF16)
            first = (nn(table[...], enc) * (1.0 / k_g)).astype(BF16)
            keep[b] = first
            hat, _ = norm_parts(first.astype(F32))
            normed[0, b] = (hat * gain).astype(BF16)

    def n_copy(layer, b):
        return remote(
            n_own.at[layer, b, :, mine], n_prev.at[layer, b, :, mine], s_n.at[layer, b], r_n.at[layer, b], after
        )

    def n_forward(layer, b, which):
        there = n_prev.at[layer, b, :, which]
        return remote(there, there, s_nf.at[layer, b], r_nf.at[layer, b], partner)

    def mix_copy(layer, b):
        return remote(
            mixed.at[layer, b, j], mixed.at[layer, b, j], s_mix.at[layer, b], r_mix.at[layer, b], partner
        )

    def mix_wait(layer, b):
        there = mixed.at[layer, b, other]
        remote(there, there, s_mix.at[layer, b], r_mix.at[layer, b], partner).wait_recv()

    scale = float(width // sz.heads) ** -0.5

    def spot(layer, b):
        return layer * nb + (b if layer < sz.layers - 1 else 0)

    def entry(layer, b):
        if layer == 0:
            return start[b].astype(F32)
        return state[layer - 1, b]

    def project(layer, b):
        base = 1 + 6 * layer
        if layer > 0:
            hat, _ = norm_parts(state[layer - 1, b])
            n_own[layer, b] = (hat * gain_row(2 * layer)).astype(BF16)
            n_copy(layer, b).start()
        normed = n_own[layer, b]
        query[layer, b] = nn(normed, w_cols(base, mine)).astype(BF16)
        pair[layer, b, 0, 0:rows] = nn(normed, w_cols(base + 1, mine)).astype(BF16)
        pair[layer, b, 1, 0:rows] = nn(normed, w_cols(base + 2, mine)).astype(BF16)

    def take_prev(layer, b):
        if layer > 0:
            n_copy(layer, b).wait_recv()
            n_forward(layer, b, mine).start()

    def attend(layer, b):
        base = 1 + 6 * layer
        if layer > 0:
            n_forward(layer, b, theirs).wait_recv()
        normed = n_prev[layer, b]
        pair[layer, b, 0, rows : 2 * rows] = nn(normed, w_cols(base + 1, mine)).astype(BF16)
        pair[layer, b, 1, rows : 2 * rows] = nn(normed, w_cols(base + 2, mine)).astype(BF16)
        keys, values, queries = pair[layer, b, 0], pair[layer, b, 1], query[layer, b]
        out = jnp.zeros((rows, cols), F32)
        for head in range(sz.near):
            score = nt(queries * mask_low[head], keys) * scale + edge_bias[...]
            expo = jnp.exp(score - jnp.max(score, axis=-1, keepdims=True))
            weight = (expo * (1.0 / jnp.sum(expo, axis=-1, keepdims=True))).astype(BF16)
            prob[layer, b, head] = weight
            out = out + nn(weight, values) * mask_full[head]
        mixed[layer, b, j] = out.astype(BF16)
        mix_copy(layer, b).start()

    def mlp(layer, b):
        base = 1 + 6 * layer
        mix_wait(layer, b)
        mid = (
            entry(layer, b)
            + nn(mixed[layer, b, 0], w_rows(base + 3, 0))
            + nn(mixed[layer, b, 1], w_rows(base + 3, 1))
        )
        middle[spot(layer, b)] = mid
        hat, _ = norm_parts(mid)
        normed = (hat * gain_row(2 * layer + 1)).astype(BF16)
        pre = nn(normed, w_full(base + 4)) + bias_row(1 + 2 * layer)
        pre_mlp[spot(layer, b)] = pre
        act = (pre * sigmoid(pre)).astype(BF16)
        state[layer, b] = mid + nn(act, w_full(base + 5)) + bias_row(2 + 2 * layer)

    last = sz.layers - 1
    lane_out = lax.broadcasted_iota(jnp.int32, (1, 128), 1)
    row_index = lax.broadcasted_iota(jnp.int32, (rows, 1), 0)
    own_row = jnp.logical_and(row_index >= j * half, row_index < (j + 1) * half).astype(F32)
    real_lane = (lane_out < sz.c_out).astype(F32)

    def decode(b):
        gain = gain_row(2 * sz.layers)
        dec = (nn(m_row[...], state[last, b].astype(BF16)) * (1.0 / k_m)).astype(BF16).astype(F32)
        hat, inv = norm_parts(dec)
        normed = (hat * gain).astype(BF16)
        final[b] = normed
        weights = aux(out_cols, 128)
        goal = rows_in[b, :, :, 256:384].reshape(rows, 128).astype(F32)
        error = (nn(normed, weights) - goal) * real_lane
        weight = goal[:, 125:126] + goal[:, 126:127] + goal[:, 127:128]
        loss_acc[...] = loss_acc[...] + jnp.sum(
            jnp.sum((weight * own_row) * error * error, axis=1, keepdims=True), axis=0, keepdims=True
        )
        pred_low = (2.0 * weight * error / scalars[1, 0:1, 0:1]).astype(BF16)
        grad_pred[b] = pred_low
        back = nt(pred_low, weights)
        add_affine(2 * sz.layers, column_sum(back * hat))
        dec_low = norm_back(back, hat, inv, gain).astype(BF16)
        state[last, b] = (nn(m_col[...], dec_low) * (1.0 / k_m)).astype(BF16).astype(F32)

    if sz.fused:
        lane_a = pl.ds(0, cols // 2)
        lane_b = pl.ds(cols // 2, cols // 2)
        lanes = (lane_a, lane_b)
        top = 32767.0

        def encoded(value, code_ref, scale_ref):
            size = jnp.max(jnp.abs(value), axis=tuple(range(value.ndim - 1)), keepdims=True)
            size = size.reshape(1, size.shape[-1])
            inverse = jnp.where(size > 1e-30, top / jnp.maximum(size, 1e-30), 0.0)
            code_ref[...] = jnp.round(value * inverse).astype(jnp.int32).astype(jnp.int16)
            scale_ref[...] = jnp.broadcast_to(size * (1.0 / top), scale_ref.shape)

        def decoded(code, scale_row):
            return code.astype(jnp.int32).astype(F32) * scale_row

        def over(unit, body):
            first, count = sz.units[unit]

            def wrapped(m, carry):
                body(m)
                return carry

            lax.fori_loop(first, first + count, wrapped, 0)

        def send_codes(unit, stage, side, device):
            span = pl.ds(*sz.units[unit])
            codes_out, codes_in = ((code_one, got_one), (code_two, got_two))[stage]

            def make_codes():
                k = 2 * stage
                return remote(
                    codes_out.at[side, span], codes_in.at[side, span], rr_s.at[unit, k, side], rr_r.at[unit, k, side], device
                )

            def make_scales():
                k = 2 * stage + 1
                return remote(
                    size_out.at[stage, side, span],
                    size_in.at[stage, side, span],
                    rr_s.at[unit, k, side],
                    rr_r.at[unit, k, side],
                    device,
                )

            return make_codes, make_scales

        def reduce_one(unit):
            def body(m):
                encoded(total[m, :, 1 - x, :, :, :, lane_a], code_one.at[0, m], size_out.at[0, 0, m])
                encoded(total[m, :, :, :, 1 - y, :, lane_b], code_one.at[1, m], size_out.at[0, 1, m])

            over(unit, body)
            for side, device in ((0, x_dev), (1, y_dev)):
                for make in send_codes(unit, 0, side, device):
                    push(make)

        def reduce_two(unit):
            for side, device in ((0, x_dev), (1, y_dev)):
                for make in send_codes(unit, 0, side, device):
                    make().wait_recv()

            def body(m):
                row_a = size_in[0, 0, m, 0:1, :]
                row_b = size_in[0, 1, m, 0:1, :]
                total[m, :, x, :, :, :, lane_a] = total[m, :, x, :, :, :, lane_a] + decoded(got_one[0, m], row_a)
                total[m, :, :, :, y, :, lane_b] = total[m, :, :, :, y, :, lane_b] + decoded(got_one[1, m], row_b)
                encoded(total[m, :, x, :, 1 - y, :, lane_a], code_two.at[0, m], size_out.at[1, 0, m])
                encoded(total[m, :, 1 - x, :, y, :, lane_b], code_two.at[1, m], size_out.at[1, 1, m])

            over(unit, body)
            for side, device in ((0, y_dev), (1, x_dev)):
                for make in send_codes(unit, 1, side, device):
                    push(make)

        def send_z(unit, step):
            span = pl.ds(*sz.units[unit])

            def make_codes():
                return remote(
                    code_z.at[span, lax.rem(z + step, depth)],
                    got_z.at[step - 1, span],
                    rz_s.at[unit, 0, step - 1],
                    rz_r.at[unit, 0, step - 1],
                    z_devs[step - 1],
                )

            def make_scales():
                return remote(
                    size_z.at[span],
                    size_z_in.at[step - 1, span],
                    rz_s.at[unit, 1, step - 1],
                    rz_r.at[unit, 1, step - 1],
                    z_devs[step - 1],
                )

            return make_codes, make_scales

        def reduce_three(unit):
            for side, device in ((0, y_dev), (1, x_dev)):
                for make in send_codes(unit, 1, side, device):
                    make().wait_recv()

            def body(m):
                for side in range(2):
                    row = size_in[1, side, m, 0:1, :]
                    total[m, :, x, :, y, :, lanes[side]] = total[m, :, x, :, y, :, lanes[side]] + decoded(
                        got_two[side, m], row
                    )
                encoded(total[m, :, x, :, y], code_z.at[m], size_z.at[m])

            over(unit, body)
            for step in range(1, depth):
                for make in send_z(unit, step):
                    push(make)

        def core_copy(unit):
            span = pl.ds(*sz.units[unit])
            return remote(total.at[span, z, x, 1 - c, y], got_c.at[span], rc_s.at[unit], rc_r.at[unit], partner)

        def reduce_four(unit):
            for step in range(1, depth):
                for make in send_z(unit, step):
                    make().wait_recv()

            def body(m):
                acc = total[m, z, x, :, y]
                for step in range(1, depth):
                    acc = acc + decoded(got_z[step - 1, m], size_z_in[step - 1, m, 0:1, :])
                total[m, z, x, :, y] = acc

            over(unit, body)
            push(lambda: core_copy(unit))

        def reduce_done(unit):
            core_copy(unit).wait_recv()

            def body(m):
                share[m, :, mine] = total[m, z, x, c, y]
                share[m, :, theirs] = got_c[m]

            over(unit, body)

        stages = (None, reduce_one, reduce_two, reduce_three, reduce_four, reduce_done)

    def summed(stage, unit):
        if sz.fused:
            stages[stage](unit)

    def far_copy(layer, b):
        return remote(d_own.at[b], d_far.at[b], s_far.at[layer, b], r_far.at[layer, b], partner)

    def dn_copy(layer, b):
        return remote(
            dn_out.at[layer - 1, b],
            dn_in.at[layer - 1, b, :, mine],
            s_dn.at[layer, b],
            r_dn.at[layer, b],
            before,
        )

    def dn_forward(layer, b, which):
        there = dn_in.at[layer - 1, b, :, which]
        return remote(there, there, s_df.at[layer, b], r_df.at[layer, b], partner)

    def mlp_back(layer, b):
        base = 1 + 6 * layer
        grad = state[last, b]
        grad_low = grad.astype(BF16)
        low[b] = grad_low
        add_affine(8 + 2 + 2 * layer, column_sum(grad))
        pre = pre_mlp[spot(layer, b)]
        gate = sigmoid(pre)
        hidden[b] = (pre * gate).astype(BF16)
        back = (nt(grad_low, w_full(base + 5)) * (gate * (1.0 + pre * (1.0 - gate)))).astype(BF16)
        pre_low[b] = back
        add_affine(8 + 1 + 2 * layer, column_sum(back.astype(F32)))
        back = nt(back, w_full(base + 4))
        gain = gain_row(2 * layer + 1)
        hat, inv = norm_parts(middle[spot(layer, b)])
        n_two[b] = (hat * gain).astype(BF16)
        add_affine(2 * layer + 1, column_sum(back * hat))
        grad = grad + norm_back(back, hat, inv, gain)
        state[last, b] = grad
        mid_low[b] = grad.astype(BF16)

    def attend_back(layer, b):
        base = 1 + 6 * layer
        grad_out = nt(mid_low[b], w_rows(base + 3, j)).astype(BF16)
        keys, values, queries = pair[layer, b, 0], pair[layer, b, 1], query[layer, b]
        d_query = jnp.zeros((rows, cols), F32)
        d_keys = jnp.zeros((2 * rows, cols), F32)
        d_values = jnp.zeros((2 * rows, cols), F32)
        for head in range(sz.near):
            weight_low = prob[layer, b, head]
            out_head = grad_out * mask_low[head]
            weight = weight_low.astype(F32)
            part = weight * nt(out_head, values)
            score = (part - weight * jnp.sum(part, axis=-1, keepdims=True)).astype(BF16)
            d_query = d_query + nn(score, keys) * mask_full[head]
            d_keys = d_keys + tn(score, queries * mask_low[head])
            d_values = d_values + tn(weight_low, out_head)
        d_keys = (d_keys * scale).astype(BF16)
        d_values = d_values.astype(BF16)
        d_own[b, :, 0:cols] = (d_query * scale).astype(BF16)
        d_own[b, :, cols : 2 * cols] = d_keys[0:rows]
        d_own[b, :, 2 * cols : 3 * cols] = d_values[0:rows]
        d_own[b, :, 3 * cols : 4 * cols] = d_keys[rows:]
        d_own[b, :, 4 * cols : 5 * cols] = d_values[rows:]
        if layer < last:
            pl.semaphore_wait(far_free, 1)
        far_copy(layer, b).start()

    def send_prev(layer, b):
        base = 1 + 6 * layer
        far_copy(layer, b).wait()
        back = jnp.zeros((rows, cols), F32)
        for which in (1, 2):
            part = pl.ds((which + 2) * cols, cols)
            back = back + nt(d_own[b, :, part], w_block(base + which, j, mine))
            back = back + nt(d_far[b, :, part], w_block(base + which, j, theirs))
        dn_out[layer - 1, b] = back.astype(BF16)
        dn_copy(layer, b).start()

    def take_next(layer, b):
        dn_copy(layer, b).wait_recv()
        dn_forward(layer, b, mine).start()

    def join(layer, b):
        base = 1 + 6 * layer
        if layer > 0:
            dn_forward(layer, b, theirs).wait_recv()
            back = dn_in[layer - 1, b].astype(F32)
        else:
            far_copy(layer, b).wait()
            back = jnp.zeros((rows, width), F32)
        for which in range(3):
            part = pl.ds(which * cols, cols)
            back = back + nt(d_own[b, :, part], w_cols(base + which, mine))
            back = back + nt(d_far[b, :, part], w_cols(base + which, theirs))
        if layer > 0:
            pl.semaphore_signal(far_free, inc=1, device_id=partner, device_id_type=MESH)
        gain = gain_row(2 * layer)
        hat, inv = norm_parts(entry(layer, b))
        add_affine(2 * layer, column_sum(back * hat))
        state[last, b] = state[last, b] + norm_back(back, hat, inv, gain)

    many = nb * rows

    def outer_mlp(layer):
        base = 1 + 6 * layer
        put_total(base + 5, tn(hidden[...].reshape(many, width), low[:, :, mine].reshape(many, cols)))
        put_total(base + 4, tn(n_two[...].reshape(many, width), pre_low[:, :, mine].reshape(many, cols)))

    def outer_mixed(layer):
        base = 1 + 6 * layer
        grad_mid = mid_low[:, :, mine].reshape(many, cols)
        put_total(
            base + 3,
            jnp.concatenate(
                [
                    tn(mixed[layer, :, 0].reshape(many, cols), grad_mid),
                    tn(mixed[layer, :, 1].reshape(many, cols), grad_mid),
                ],
                axis=0,
            ),
        )

    def outer_pair(layer):
        base = 1 + 6 * layer
        near = tn(n_own[layer].reshape(many, width), d_own[:, :, 0 : 3 * cols].reshape(many, 3 * cols))
        put_total(base, near[:, 0:cols])
        away = tn(n_prev[layer].reshape(many, width), d_own[:, :, 3 * cols : 5 * cols].reshape(many, 2 * cols))
        put_total(base + 1, near[:, cols : 2 * cols] + away[:, 0:cols])
        put_total(base + 2, near[:, 2 * cols : 3 * cols] + away[:, cols : 2 * cols])

    def encode_back(b):
        back = nn(g_col[...], state[last, b].astype(BF16)) * (1.0 / k_g)
        back = (back.astype(BF16).astype(F32) * silu_slope(pre_encode(rows_in, b))).astype(BF16)
        low[b] = back
        add_affine(8, column_sum(back.astype(F32)))
        back = jnp.zeros((rows, width), F32)
        for which in (1, 2):
            part = pl.ds((which + 2) * cols, cols)
            back = back + nt(d_own[b, :, part], w_cols(1 + which, mine))
            back = back + nt(d_far[b, :, part], w_cols(1 + which, theirs))
        gain = gain_row(0)
        hat, inv = norm_parts(start_prev[b].astype(F32))
        add_affine(0, column_sum(back * hat))
        back = nn(gp_col[...], norm_back(back, hat, inv, gain).astype(BF16)) * (1.0 / k_g)
        back = (back.astype(BF16).astype(F32) * silu_slope(pre_encode(rows_prev, b))).astype(BF16)
        mid_low[b] = back
        add_affine(8, column_sum(back.astype(F32)))

    each(encode)
    gathered(3, 2)
    gathered(2, 3)
    gathered(5, 1)

    def first_project(b):
        project(0, b)

    each(first_project)
    gathered(4, 2)
    gathered(3, 3)
    gathered(2, 4)
    for layer in range(last):

        def attend_this(b, layer=layer):
            take_prev(layer, b)
            attend(layer, b)

        def mlp_this(b, layer=layer):
            mlp(layer, b)

        def project_next(b, layer=layer):
            project(layer + 1, b)

        def ready(g=2 * layer):
            gathered(5, g + 2)
            gathered(4, g + 3)
            gathered(3, g + 4)

        def ready_next(g=2 * layer):
            gathered(5, g + 3)
            gathered(4, g + 4)

        staggered(attend_this, mlp_this, project_next, hooks=(None, ready, ready_next))
        gathered(2, 2 * layer + 5)
        gathered(3, 2 * layer + 5)
        gathered(2, 2 * layer + 6)
        gathered(4, 2 * layer + 5)
        gathered(3, 2 * layer + 6)

    def ready_last():
        if last == 0:
            gathered(4, 2)
        gathered(5, 2 * last + 2)
        scalars[1] = tile_end(0) if sz.fused else jnp.broadcast_to(weight_ref[...], (8, 128))

    def attend_last(b):
        take_prev(last, b)
        attend(last, b)

    def turn(b):
        mlp(last, b)
        decode(b)
        mlp_back(last, b)
        attend_back(last, b)

    def send_last(b):
        if last > 0:
            send_prev(last, b)

    staggered(attend_last, turn, send_last, hooks=(None, ready_last))
    outer_mlp(last)
    summed(1, 2 * last + 2)
    outer_mixed(last)
    outer_pair(last)
    summed(1, 2 * last + 1)
    for layer in reversed(range(last)):

        def take_this(b, layer=layer):
            take_next(layer + 1, b)

        each(take_this)

        def back_this(b, layer=layer):
            join(layer + 1, b)
            mlp_back(layer, b)

        def pair_this(b, layer=layer):
            attend_back(layer, b)

        def send_this(b, layer=layer):
            if layer > 0:
                send_prev(layer, b)

        u = 2 * layer
        each(back_this, hooks=(None, lambda u=u: summed(2, u + 4), lambda u=u: summed(2, u + 3)))
        outer_mlp(layer)
        summed(1, u + 2)
        summed(3, u + 4)
        hooks = (None, lambda u=u: summed(2, u + 2), lambda u=u: summed(3, u + 3))
        if layer > 0:
            staggered(pair_this, send_this, hooks=hooks)
        else:
            each(pair_this, hooks=hooks)
        outer_mixed(layer)
        outer_pair(layer)
        summed(1, u + 1)
        summed(4, u + 4)
        if layer > 0:
            summed(4, u + 3)

    def last_back(b):
        join(0, b)
        encode_back(b)

    each(last_back, hooks=(None, lambda: summed(3, 2), lambda: summed(2, 1)))
    wide = jnp.concatenate([affine_grad[...], jnp.zeros((112, width), F32)], axis=0)

    @pl.when(j == 0)
    def _():
        put_total(
            0,
            tn(low[...].reshape(many, width), rows_in[:, :, :, 0:256].reshape(many, 256))
            + tn(mid_low[...].reshape(many, width), rows_prev[...].reshape(many, 256)),
        )

    @pl.when(j == 1)
    def _():
        put_total(
            0,
            jnp.concatenate(
                [
                    jnp.transpose(wide),
                    tn(final[...].reshape(many, width), grad_pred[...].reshape(many, 128)),
                ],
                axis=1,
            ),
        )

    if sz.fused:
        reduce_one(0)
        if sz.layers > 1:
            reduce_four(3)
        reduce_three(1)
        reduce_two(0)
        reduce_four(2)
        reduce_three(0)
        for unit in range(2, len(sz.units)):
            reduce_done(unit)
        reduce_four(1)
        reduce_four(0)
        reduce_done(1)
        reduce_done(0)
        squares = jnp.zeros((1, 1), F32)
        for index in range(sz.mats):
            value = share[index]
            squares = squares + jnp.sum(
                jnp.sum(value * value, axis=1, keepdims=True), axis=0, keepdims=True
            )
        sub = lax.broadcasted_iota(jnp.int32, (8, 128), 0)
        tile[1, 0] = jnp.where(sub == 0, squares, loss_acc[0:1, 0:1])
        tile_start(1)
        result = tile_end(1)
        scalars[0] = jnp.broadcast_to(result[1:2, :], (8, 128))
        scalars[2] = jnp.broadcast_to(jnp.sqrt(result[0:1, :]), (8, 128))
    else:
        scalars[0] = loss_acc[...]
        scalars[2] = loss_acc[...]

    for make in waits:
        make().wait_send()
    for layer in range(sz.layers):
        for b in range(nb):
            mix_copy(layer, b).wait_send()
            if layer > 0:
                n_copy(layer, b).wait_send()
                n_forward(layer, b, mine).wait_send()
                dn_copy(layer, b).wait_send()
                dn_forward(layer, b, mine).wait_send()


def dma(*shape):
    return pltpu.SemaphoreType.DMA(shape)


def train_kernel(sz, operands):
    nb, rows, half, width, cols = sz.batches, sz.rows, sz.half, sz.width, sz.cols
    layers = sz.layers
    scratch = []
    if sz.fused:
        out_shape = (
            jax.ShapeDtypeStruct((sz.mats, sz.shard, width), F32),
            jax.ShapeDtypeStruct((3, 8, 128), F32),
        )
        scratch += [
            pltpu.VMEM((sz.mats, sz.depth, 2, 2, 2, sz.shard, width), BF16),
            pltpu.VMEM((sz.mats, sz.depth, 2, 2, 2, sz.shard, cols), F32),
        ]
    else:
        out_shape = (
            jax.ShapeDtypeStruct((sz.mats, width, cols), F32),
            jax.ShapeDtypeStruct((3, 8, 128), F32),
        )
    scratch += [
        pltpu.VMEM((nb, half, 384), BF16),
        pltpu.VMEM((nb, 2, half, 384), BF16),
        pltpu.VMEM((nb, 2, half, 256), BF16),
        pltpu.VMEM((3, 32, rows), jnp.int32),
        pltpu.VMEM((nb, rows, width), BF16),
        pltpu.VMEM((nb, rows, width), BF16),
        pltpu.VMEM((layers, nb, rows, width), F32),
        pltpu.VMEM(((layers - 1) * nb + 1, rows, width), F32),
        pltpu.VMEM(((layers - 1) * nb + 1, rows, width), F32),
        pltpu.VMEM((layers, nb, 2, rows, cols), BF16),
        pltpu.VMEM((layers, nb, rows, cols), BF16),
        pltpu.VMEM((layers, nb, 2, 2 * rows, cols), BF16),
        pltpu.VMEM((layers, nb, sz.near, rows, 2 * rows), BF16),
        pltpu.VMEM((rows, 2 * rows), F32),
    ]
    scratch += [pltpu.VMEM((rows, rows), BF16)] * 6
    scratch += [pltpu.VMEM((16, width), F32)] * 2
    scratch += [
        pltpu.VMEM((nb, rows, width), BF16),
        pltpu.VMEM((nb, rows, 128), BF16),
        pltpu.VMEM((nb, rows, width), BF16),
        pltpu.VMEM((nb, rows, width), BF16),
        pltpu.VMEM((nb, rows, width), BF16),
        pltpu.VMEM((layers, nb, rows, width), BF16),
        pltpu.VMEM((layers, nb, rows, width), BF16),
        pltpu.VMEM((nb, rows, width), BF16),
        pltpu.VMEM((nb, rows, width), BF16),
        pltpu.VMEM((nb, rows, 5 * cols), BF16),
        pltpu.VMEM((nb, rows, 5 * cols), BF16),
        pltpu.VMEM((max(layers - 1, 1), nb, rows, cols), BF16),
        pltpu.VMEM((max(layers - 1, 1), nb, rows, width), BF16),
        pltpu.VMEM((8, 128), F32),
    ]
    scratch += [dma(3), dma(3), dma(2), dma(2), dma(2), dma(2)] + [dma(layers, nb)] * 12
    scratch += [pltpu.SemaphoreType.REGULAR]
    if sz.fused:
        depth, groups, units = sz.depth, len(sz.groups), len(sz.units)
        lane = cols // 2
        one_shape = (2, sz.mats, depth, 2, 2, sz.shard, lane)
        two_shape = (2, sz.mats, depth, 2, sz.shard, lane)
        scratch += [pltpu.VMEM(one_shape, jnp.int16)] * 2 + [pltpu.VMEM(two_shape, jnp.int16)] * 2
        scratch += [
            pltpu.VMEM((sz.mats, depth, 2, sz.shard, cols), jnp.int16),
            pltpu.VMEM((depth - 1, sz.mats, 2, sz.shard, cols), jnp.int16),
            pltpu.VMEM((sz.mats, sz.shard, cols), F32),
            pltpu.VMEM((2, 2, sz.mats, 8, lane), F32),
            pltpu.VMEM((2, 2, sz.mats, 8, lane), F32),
            pltpu.VMEM((sz.mats, 8, cols), F32),
            pltpu.VMEM((depth - 1, sz.mats, 8, cols), F32),
            pltpu.VMEM((2, 2, 8, 128), F32),
            pltpu.VMEM((2, 8, 128), F32),
            pltpu.VMEM((2, 4 * depth, 8, 128), F32),
        ]
        far = [dma(groups, depth - 1)] * 2
        scratch += far + [dma(groups, 2)] * 4 + [dma(groups)] * 2
        scratch += [dma(units, 4, 2)] * 2 + [dma(units, 2, depth - 1)] * 2 + [dma(units)] * 2
        scratch += [dma(2)] * 2 + [dma(2, 4 * depth - 1)] * 2
    return pl.pallas_call(
        functools.partial(step_kernel, sz),
        out_shape=out_shape,
        in_specs=[pl.BlockSpec(memory_space=pltpu.VMEM)] * len(operands),
        out_specs=(pl.BlockSpec(memory_space=pltpu.VMEM),) * 2,
        scratch_shapes=scratch,
        compiler_params=pltpu.CompilerParams(
            collective_id=0, has_side_effects=True, vmem_limit_bytes=60 * 1024 * 1024
        ),
    )(*operands)


def adam(weight, first, second, grad):
    first_new = BETA_ONE * first + (1.0 - BETA_ONE) * grad
    second_new = BETA_TWO * second + (1.0 - BETA_TWO) * grad * grad
    first_hat = first_new / (1.0 - BETA_ONE**STEP)
    second_hat = second_new / (1.0 - BETA_TWO**STEP)
    weight_new = weight - RATE * (first_hat / (jnp.sqrt(second_hat) + ADAM_EPS) + DECAY * weight)
    return (weight_new, first_new, second_new, weight_new.astype(BF16))


def adam_kernel(sz, share, scalars, *refs):
    masters = refs[:15]
    outs = refs[15:35]
    mat, inp, out, gain, bias = [masters[3 * k : 3 * k + 3] for k in range(5)]
    factor = jnp.minimum(1.0, CLIP / (scalars[2, 0:1, 0:1] + 1e-06))

    def put(k, values):
        for ref, value in zip(outs[4 * k : 4 * k + 4], values):
            ref[...] = value

    for index in range(sz.mats - 1):
        values = adam(mat[0][index], mat[1][index], mat[2][index], factor * share[1 + index])
        for ref, value in zip(outs[0:4], values):
            ref[index] = value
    last = share[0]
    put(1, adam(inp[0][...], inp[1][...], inp[2][...], factor * last[:, 0 : sz.c_in]))
    put(2, adam(out[0][...], out[1][...], out[2][...], factor * last[:, 384 : 384 + sz.c_out]))
    small = jnp.concatenate([last[:, 256:384], jnp.zeros((128 - sz.shard, 128), F32)], axis=0)
    small = jnp.transpose(small)[:, 0 : sz.shard]
    count = gain[0].shape[0]
    put(3, adam(gain[0][...], gain[1][...], gain[2][...], factor * small[0:count]))
    put(4, adam(bias[0][...], bias[1][...], bias[2][...], factor * small[8 : 8 + count]))


def update(sz, share, scalars, groups):
    operands = [share, scalars]
    out_shape = []
    for triple in groups:
        operands += list(triple)
        shape = triple[0].shape
        out_shape += [jax.ShapeDtypeStruct(shape, F32)] * 3 + [jax.ShapeDtypeStruct(shape, BF16)]
    return pl.pallas_call(
        functools.partial(adam_kernel, sz),
        out_shape=tuple(out_shape),
        in_specs=[pl.BlockSpec(memory_space=pltpu.VMEM)] * len(operands),
        out_specs=(pl.BlockSpec(memory_space=pltpu.VMEM),) * len(out_shape),
    )(*operands)


def per_device(
    grid_in, targets, area, row_count, g2m, m2g, senders, edge_count,
    mat_w, mat_m, mat_v, in_w, in_m, in_v, out_w, out_m, out_v,
    gain_w, gain_m, gain_v, bias_w, bias_m, bias_v,
):
    axes = ("node", "feat")
    sz = Sizes(
        lax.axis_size("node"),
        lax.axis_size("feat"),
        grid_in.shape[0],
        grid_in.shape[1],
        mat_w.shape[2],
        mat_w.shape[0] // 6,
        HEADS,
        senders.shape[1],
        grid_in.shape[2],
        targets.shape[2],
    )
    operands = [
        jnp.swapaxes(grid_in, 1, 2),
        jnp.swapaxes(targets, 1, 2),
        area.reshape(1, -1),
        row_count,
        g2m.T,
        m2g.T,
        senders.T,
        edge_count.reshape(1, -1),
    ]
    if sz.fused:
        operands += [mat_w, in_w.T, out_w, gain_w, bias_w]
        share, scalars = train_kernel(sz, operands)
        groups = (
            (mat_w, mat_m, mat_v),
            (in_w.T, in_m.T, in_v.T),
            (out_w, out_m, out_v),
            (gain_w, gain_m, gain_v),
            (bias_w, bias_m, bias_v),
        )
        outs = list(update(sz, share, scalars, groups))
        for index in range(4, 8):
            outs[index] = outs[index].T
        return tuple(outs) + (scalars[0, 0, 0], scalars[1, 0, 0], scalars[2, 0, 0])

    width, shard = sz.width, sz.shard

    def pad(value, size):
        return jnp.pad(value, ((0, 0), (0, size - value.shape[1])))

    def pack(square, inp, out, gain, bias):
        small = jnp.concatenate([pad(gain.T, 8), pad(bias.T, 120)], axis=1)
        first = jnp.concatenate([pad(inp.T, 256), small, pad(out, 128)], axis=1)
        return jnp.concatenate([first[None], square], axis=0)

    packed = pack(mat_w, in_w, out_w, gain_w, bias_w).astype(BF16)
    full = lax.all_gather(packed, axes, axis=1, tiled=True).reshape(sz.mats, 2, width // 2, width)
    live = (jnp.arange(sz.half)[None, :] < row_count).astype(F32)
    weight_total = lax.psum(jnp.sum(area[None, :] * live) * targets.shape[2], axes)
    operands += [full, weight_total.reshape(1, 1)]
    part, scalars = train_kernel(sz, operands)
    feat = lax.axis_index("feat")
    spread = lax.dynamic_update_slice(
        jnp.zeros((sz.mats, width, width), F32), part, (0, 0, feat * sz.cols)
    )
    share = lax.psum_scatter(spread, axes, scatter_dimension=1, tiled=True)
    square_sum, loss_sum = lax.psum((jnp.sum(share * share), scalars[0, 0, 0]), axes)
    grad_norm = jnp.sqrt(square_sum)
    share = jnp.minimum(1.0, CLIP / (grad_norm + 1e-06)) * share
    count = gain_w.shape[0]
    last = share[0]
    outs = adam(mat_w, mat_m, mat_v, share[1:])
    outs += adam(in_w, in_m, in_v, last[:, 0 : sz.c_in].T)
    outs += adam(out_w, out_m, out_v, last[:, 384 : 384 + sz.c_out])
    outs += adam(gain_w, gain_m, gain_v, last[:, 256 : 256 + count].T)
    outs += adam(bias_w, bias_m, bias_v, last[:, 264 : 264 + count].T)
    return outs + (loss_sum, weight_total, grad_norm)


def solution(mesh):
    both = ("node", "feat")
    rows_three = P(None, both, None)
    second = P(None, both)
    first = P(both, None)
    placed = (
        rows_three, rows_three, P(both), second,
        P("node", None), P("node", None), P("node", None), P("node"),
    )
    placed += (rows_three,) * 3 + (second,) * 3 + (first,) * 3 + (second,) * 6
    outs = (rows_three,) * 4 + (second,) * 4 + (first,) * 4 + (second,) * 8 + (P(), P(), P())
    return jax.shard_map(per_device, mesh=mesh, in_specs=placed, out_specs=outs, check_vma=False)
```

time: 216 us -> 163 us (0.75)
  Pallas kernels: 213 us -> 159 us
    pallas_call x1, Pallas kernels: 210 us -> 156 us  [train_kernel(): pl.pallas_call(functools.partial(step_kernel, sz), out_shape=out_shape, i...]
where the time goes in v2:
time: 163 us
  Pallas kernels  159 us (98%)
  local copies, waits for them, and re-layouts  2.52 us (2%)
    pallas_call x1, Pallas kernels, train_kernel(): pl.pallas_call(functools.partial(step_kernel, sz), out_shape=out_shape, i...  156 us

profile of v2, /device:TPU:0, one launch (start us, length us, event | category | flops | bytes accessed | tf_op | source)
XLA Modules:
  0.0 162.6 jit_solution(8510943717251940761)
XLA Ops:
  0.7 0.0 copy-start
  0.7 0.6 copy-done
  1.3 0.7 copy.46.refs_3_
  2.0 156.4 %shard_map.398 = (f32[13,16,512]{2,1,0:T(8,128)}, f32[3,8,128]{2,1,0:T(8,128)}) custom-call(bf16[3,227,128]{2,1,0:T(8,128)(2,1)} %bitcast.17, bf16[3,83,128]{2,1,0:T(8,128)(2,1)} %bitcast.18, f32[1,128]{1,0:T(1,128)} %bitcast.26, s32[3,1]{1,0:T(4,128)} %copy.46.refs_3_, s32[8,256]{1,0:T(8,128)} %bitcast.24, s32[3,256]{1,0:T(4,128)} %bitcast.25, ...), custom_call_target="tpu_custom_call" | custom-call | tf_op jit(solution)/shard_map/pallas_call | solution.py:1185
  158.4 2.9 %shard_map.399 = (f32[12,16,512]{2,1,0:T(8,128)}, f32[12,16,512]{2,1,0:T(8,128)}, f32[12,16,512]{2,1,0:T(8,128)}, bf16[12,16,512]{2,1,0:T(8,128)(2,1)}, f32[16,2...) custom-call(f32[13,16,512]{2,1,0:T(8,128)} %get-tuple-element.45.sha, ...), custom_call_target="tpu_custom_call" | custom-call | tf_op jit(solution)/shard_map/pallas_call | solution.py:1237
  161.4 1.2 fusion
Async XLA Ops:
  0.7 0.7 copy-start

commit v3 on v2

--- a/solution.py
+++ b/solution.py
@@ -53,7 +53,7 @@
 
 
 def sigmoid(value):
-    return 1.0 / (1.0 + jnp.exp(-value))
+    return 0.5 * jnp.tanh(0.5 * value) + 0.5
 
 
 def silu_slope(value):
@@ -74,10 +74,10 @@
         self.cols = width // feat
         self.near = heads // feat
         self.fused = self.shard % 16 == 0 and node % 4 == 0
-        self.groups = [(0, 1)] + [(first, 3) for first in range(1, self.mats, 3)]
+        self.groups = [(0, 1)] + [(first, 2) for first in range(1, self.mats, 2)]
         self.units = [(0, 1)]
         for layer in range(layers):
-            self.units += [(1 + 6 * layer, 4), (5 + 6 * layer, 2)]
+            self.units += [(1 + 6 * layer, 3), (4 + 6 * layer, 3)]
 
 
 def step_kernel(sz, *refs):
@@ -93,6 +93,20 @@
         mat_ref, in_ref, out_ref, gain_ref, bias_ref = take(5)
         share, scalars = take(2)
         full, total = take(2)
+        held = take(13)
+        (in_sems,) = take(1)
+        incoming = [
+            pltpu.make_async_copy(src, dst, in_sems.at[k])
+            for k, (src, dst) in enumerate(
+                zip(
+                    (grid_ref, target_ref, area_ref, count_ref, g2m_ref, m2g_ref, send_ref, edge_ref)
+                    + (mat_ref, in_ref, out_ref, gain_ref, bias_ref),
+                    held,
+                )
+            )
+        ]
+        grid_ref, target_ref, area_ref, count_ref, g2m_ref, m2g_ref, send_ref, edge_ref = held[:8]
+        mat_ref, in_ref, out_ref, gain_ref, bias_ref = held[8:]
     else:
         full, weight_ref = take(2)
         total, scalars = take(2)
@@ -133,7 +147,8 @@
         dn_out,
         dn_in,
         loss_acc,
-    ) = take(36)
+        square_acc,
+    ) = take(37)
     (s_rows, r_rows, s_idx, r_idx, s_prev, r_prev) = take(6)
     (s_n, r_n, s_nf, r_nf, s_mix, r_mix, s_dn, r_dn, s_df, r_df, s_far, r_far) = take(12)
     (far_free,) = take(1)
@@ -196,7 +211,11 @@
     barrier = pltpu.get_barrier_semaphore()
     for device in greet:
         pl.semaphore_signal(barrier, inc=1, device_id=device, device_id_type=MESH)
-    pl.semaphore_wait(barrier, len(greet))
+    if sz.fused:
+        for copy in incoming:
+            copy.start()
+        for copy in incoming:
+            copy.wait()
 
     lanes_c = lax.broadcasted_iota(jnp.int32, (1, cols), 1) // (width // sz.heads)
     mask_low = [(lanes_c == head).astype(F32).astype(BF16) for head in range(sz.near)]
@@ -229,7 +248,7 @@
     for b in range(nb):
         block_in = jnp.concatenate([grid_ref[b].astype(F32), jnp.zeros((256 - sz.c_in, half), F32)], axis=0)
         rows_own[b, :, 0:256] = jnp.transpose(block_in).astype(BF16)
-        weight = jnp.where(cell < count_ref[b : b + 1, 0:1], area_ref[...], 0.0)
+        weight = jnp.where(cell < count_ref[0:1, b : b + 1], area_ref[...], 0.0)
         first = weight.astype(BF16).astype(F32)
         second = (weight - first).astype(BF16).astype(F32)
         third = weight - first - second
@@ -245,27 +264,6 @@
     indices[slot, 8 : 8 + k_m] = m2g_ref[...]
     indices[slot, 15:16] = jnp.where(receiver < rows // 2, edge_ref[0:1, 0:1], edge_ref[0:1, 1:2])
     indices[slot, 16 : 16 + sz.slots] = send_ref[...]
-    here = rows_in.at[:, y]
-    there = rows_in.at[:, 1 - y]
-    if sz.fused:
-        push(lambda: remote(indices.at[c], indices.at[c], s_idx.at[0], r_idx.at[0], partner))
-        to_partner = remote(rows_own, here, s_rows.at[0], r_rows.at[0], partner)
-        to_chip = remote(rows_own, here, s_rows.at[1], r_rows.at[1], y_dev)
-        forward = remote(there, there, s_rows.at[2], r_rows.at[1], partner)
-
-        @pl.when(c == y)
-        def _():
-            to_partner.start()
-            rows_in[:, y] = rows_own[...]
-
-        @pl.when(c != y)
-        def _():
-            to_chip.start()
-
-    else:
-        push(lambda: remote(rows_own, here, s_rows.at[0], r_rows.at[0], partner))
-        rows_in[:, y] = rows_own[...]
-
     if sz.fused:
         n_groups = len(sz.groups)
         packed = jnp.concatenate(
@@ -294,6 +292,31 @@
         for index in range(sz.mats - 1):
             full[1 + index, z, x, c, y] = mat_ref[index].astype(BF16)
 
+    pl.semaphore_wait(barrier, len(greet))
+
+    here = rows_in.at[:, y]
+    there = rows_in.at[:, 1 - y]
+    if sz.fused:
+        push(lambda: remote(indices.at[c], indices.at[c], s_idx.at[0], r_idx.at[0], partner))
+        to_partner = remote(rows_own, here, s_rows.at[0], r_rows.at[0], partner)
+        to_chip = remote(rows_own, here, s_rows.at[1], r_rows.at[1], y_dev)
+        forward = remote(there, there, s_rows.at[2], r_rows.at[1], partner)
+
+        @pl.when(c == y)
+        def _():
+            to_partner.start()
+            rows_in[:, y] = rows_own[...]
+
+        @pl.when(c != y)
+        def _():
+            to_chip.start()
+
+    else:
+        push(lambda: remote(rows_own, here, s_rows.at[0], r_rows.at[0], partner))
+        rows_in[:, y] = rows_own[...]
+
+    if sz.fused:
+
         def gather_one(g):
             first, count = sz.groups[g]
             for step in range(1, depth):
@@ -306,12 +329,11 @@
 
         gather_one(0)
         gather_one(1)
-        gather_one(2)
 
     if sz.fused:
         weight_sum = jnp.zeros((1, 1), F32)
         for b in range(nb):
-            weight = jnp.where(cell < count_ref[b : b + 1, 0:1], area_ref[...], 0.0)
+            weight = jnp.where(cell < count_ref[0:1, b : b + 1], area_ref[...], 0.0)
             weight_sum = weight_sum + jnp.sum(weight, axis=1, keepdims=True)
         tile[0, 0] = jnp.broadcast_to(weight_sum * float(sz.c_out), (8, 128))
 
@@ -350,6 +372,104 @@
         slot = y
     push(lambda: remote(indices.at[slot], indices.at[2], s_idx.at[1], r_idx.at[1], after))
 
+    affine_grad[...] = jnp.zeros_like(affine_grad)
+    loss_acc[...] = jnp.zeros_like(loss_acc)
+    square_acc[...] = jnp.zeros_like(square_acc)
+
+    if sz.fused:
+        side_a = pl.ds(0, width // 2)
+        side_b = pl.ds(width // 2, width // 2)
+
+        def gather_part(g, stage, which):
+            span = pl.ds(*sz.groups[g])
+            if stage == 2:
+                return full.at[span, :, x, c, y, :, which]
+            if which is side_a:
+                return full.at[span, :, :, c, y, :, which]
+            return full.at[span, :, x, c, :, :, which]
+
+        def gather_push(g, stage, side, sems, device):
+            which = (side_a, side_b)[side]
+
+            def make():
+                part = gather_part(g, stage, which)
+                return remote(part, part, sems[0].at[g, side], sems[1].at[g, side], device)
+
+            push(make)
+
+        def arrived(part, s_sem, r_sem, device):
+            remote(part, part, s_sem, r_sem, device).wait_recv()
+
+        def gather_two(g):
+            span = pl.ds(*sz.groups[g])
+            for step in range(1, depth):
+                there = full.at[span, lax.rem(z + depth - step, depth), x, c, y]
+                arrived(there, gz_s.at[g, step - 1], gz_r.at[g, step - 1], z_devs[step - 1])
+            gather_push(g, 2, 0, (g2_s, g2_r), x_dev)
+            gather_push(g, 2, 1, (g2_s, g2_r), y_dev)
+
+        def gather_three(g):
+            span = pl.ds(*sz.groups[g])
+            arrived(full.at[span, :, 1 - x, c, y, :, side_a], g2_s.at[g, 0], g2_r.at[g, 0], x_dev)
+            gather_push(g, 3, 0, (g3_s, g3_r), y_dev)
+            arrived(full.at[span, :, x, c, 1 - y, :, side_b], g2_s.at[g, 1], g2_r.at[g, 1], y_dev)
+            gather_push(g, 3, 1, (g3_s, g3_r), x_dev)
+
+        def gather_four(g):
+            span = pl.ds(*sz.groups[g])
+            arrived(full.at[span, :, :, c, 1 - y, :, side_a], g3_s.at[g, 0], g3_r.at[g, 0], y_dev)
+            arrived(full.at[span, :, 1 - x, c, :, :, side_b], g3_s.at[g, 1], g3_r.at[g, 1], x_dev)
+
+            def make():
+                part = full.at[span, :, :, c]
+                return remote(part, part, g4_s.at[g], g4_r.at[g], partner)
+
+            push(make)
+
+        def gather_done(g):
+            span = pl.ds(*sz.groups[g])
+            arrived(full.at[span, :, :, 1 - c], g4_s.at[g], g4_r.at[g], partner)
+
+    def gather_step(step):
+        if not sz.fused:
+            return
+        for stage, move in enumerate((gather_two, gather_three, gather_four, gather_done)):
+            if 0 <= step - stage < len(sz.groups):
+                move(step - stage)
+        if 2 <= step + 2 < len(sz.groups):
+            gather_one(step + 2)
+
+    in_cols = pl.ds(0, 256)
+    small_cols = pl.ds(256, 128)
+    out_cols = pl.ds(384, 128)
+
+    def aux(which, size):
+        if sz.fused:
+            return full[0, :, :, :, :, :, which].reshape(width, size)
+        return full[0, :, :, which].reshape(width, size)
+
+    gather_step(0)
+    if sz.fused:
+
+        @pl.when(c == y)
+        def _():
+            remote(there, there, s_rows.at[1], r_rows.at[1], y_dev).wait_recv()
+            forward.start()
+            to_partner.wait_send()
+            forward.wait_send()
+
+        @pl.when(c != y)
+        def _():
+            to_chip.wait_send()
+            remote(here, here, s_rows.at[0], r_rows.at[0], partner).wait_recv()
+            remote(there, there, s_rows.at[2], r_rows.at[1], partner).wait_recv()
+
+    else:
+        remote(there, there, s_rows.at[0], r_rows.at[0], partner).wait_recv()
+
+    push(lambda: remote(rows_in.at[:, j, :, 0:256], rows_prev.at[:, j], s_prev.at[0], r_prev.at[0], after))
+
+    gather_step(1)
     def counts(place, first, slots, origin, live=None):
         wide = lax.broadcasted_iota(jnp.int32, (rows, rows), 0) + origin
         acc = jnp.zeros((rows, rows), F32)
@@ -370,115 +490,14 @@
     table = counts(slot, 8, k_m, 0)
     m_col[...] = table.astype(BF16)
     m_row[...] = jnp.transpose(table).astype(BF16)
-    affine_grad[...] = jnp.zeros_like(affine_grad)
-    loss_acc[...] = jnp.zeros_like(loss_acc)
-
-    if sz.fused:
-
-        @pl.when(c == y)
-        def _():
-            remote(there, there, s_rows.at[1], r_rows.at[1], y_dev).wait_recv()
-            forward.start()
-            to_partner.wait_send()
-            forward.wait_send()
-
-        @pl.when(c != y)
-        def _():
-            to_chip.wait_send()
-            remote(here, here, s_rows.at[0], r_rows.at[0], partner).wait_recv()
-            remote(there, there, s_rows.at[2], r_rows.at[1], partner).wait_recv()
-
-    else:
-        remote(there, there, s_rows.at[0], r_rows.at[0], partner).wait_recv()
-
-    push(lambda: remote(rows_in.at[:, j, :, 0:256], rows_prev.at[:, j], s_prev.at[0], r_prev.at[0], after))
-
-    if sz.fused:
-        side_a = pl.ds(0, width // 2)
-        side_b = pl.ds(width // 2, width // 2)
-
-        def gather_part(g, stage, which):
-            span = pl.ds(*sz.groups[g])
-            if stage == 2:
-                return full.at[span, :, x, c, y, :, which]
-            if which is side_a:
-                return full.at[span, :, :, c, y, :, which]
-            return full.at[span, :, x, c, :, :, which]
-
-        def gather_push(g, stage, side, sems, device):
-            which = (side_a, side_b)[side]
-
-            def make():
-                part = gather_part(g, stage, which)
-                return remote(part, part, sems[0].at[g, side], sems[1].at[g, side], device)
-
-            push(make)
-
-        def arrived(part, s_sem, r_sem, device):
-            remote(part, part, s_sem, r_sem, device).wait_recv()
-
-        def gather_two(g):
-            span = pl.ds(*sz.groups[g])
-            for step in range(1, depth):
-                there = full.at[span, lax.rem(z + depth - step, depth), x, c, y]
-                arrived(there, gz_s.at[g, step - 1], gz_r.at[g, step - 1], z_devs[step - 1])
-            gather_push(g, 2, 0, (g2_s, g2_r), x_dev)
-            gather_push(g, 2, 1, (g2_s, g2_r), y_dev)
-
-        def gather_three(g):
-            span = pl.ds(*sz.groups[g])
-            arrived(full.at[span, :, 1 - x, c, y, :, side_a], g2_s.at[g, 0], g2_r.at[g, 0], x_dev)
-            gather_push(g, 3, 0, (g3_s, g3_r), y_dev)
-            arrived(full.at[span, :, x, c, 1 - y, :, side_b], g2_s.at[g, 1], g2_r.at[g, 1], y_dev)
-            gather_push(g, 3, 1, (g3_s, g3_r), x_dev)
-
-        def gather_four(g):
-            span = pl.ds(*sz.groups[g])
-            arrived(full.at[span, :, :, c, 1 - y, :, side_a], g3_s.at[g, 0], g3_r.at[g, 0], y_dev)
-            arrived(full.at[span, :, 1 - x, c, :, :, side_b], g3_s.at[g, 1], g3_r.at[g, 1], x_dev)
-
-            def make():
-                part = full.at[span, :, :, c]
-                return remote(part, part, g4_s.at[g], g4_r.at[g], partner)
-
-            push(make)
-
-        def gather_done(g):
-            span = pl.ds(*sz.groups[g])
-            arrived(full.at[span, :, :, 1 - c], g4_s.at[g], g4_r.at[g], partner)
-
-    def gathered(stage, g):
-        if sz.fused and g < len(sz.groups):
-            (None, gather_one, gather_two, gather_three, gather_four, gather_done)[stage](g)
-
-    gathered(2, 0)
-    gathered(1, 3)
-    gathered(2, 1)
-    gathered(1, 4)
-    gathered(3, 0)
-    for g in range(5, len(sz.groups)):
-        gathered(1, g)
-
-    in_cols = pl.ds(0, 256)
-    small_cols = pl.ds(256, 128)
-    out_cols = pl.ds(384, 128)
-
-    def aux(which, size):
-        if sz.fused:
-            return full[0, :, :, :, :, :, which].reshape(width, size)
-        return full[0, :, :, which].reshape(width, size)
-
+    gather_step(2)
+    remote(rows_prev.at[:, j], rows_prev.at[:, j], s_prev.at[0], r_prev.at[0], after).wait_recv()
+    push(lambda: remote(rows_prev.at[:, j], rows_prev.at[:, j], s_prev.at[1], r_prev.at[1], partner))
     remote(indices.at[slot], indices.at[2], s_idx.at[1], r_idx.at[1], after).wait_recv()
     table = counts(2, 0, k_g, 0)
     gp_col[...] = table.astype(BF16)
     gp_row[...] = jnp.transpose(table).astype(BF16)
-    remote(rows_prev.at[:, j], rows_prev.at[:, j], s_prev.at[0], r_prev.at[0], after).wait_recv()
-    push(lambda: remote(rows_prev.at[:, j], rows_prev.at[:, j], s_prev.at[1], r_prev.at[1], partner))
-    gathered(3, 1)
-    gathered(2, 2)
-    gathered(4, 0)
-    gathered(4, 1)
-    gathered(5, 0)
+    gather_step(3)
     remote(rows_prev.at[:, other], rows_prev.at[:, other], s_prev.at[1], r_prev.at[1], partner).wait_recv()
 
     affine[...] = jnp.transpose(aux(small_cols, 128).astype(F32))[0:16, :]
@@ -767,6 +786,7 @@
                 for step in range(1, depth):
                     acc = acc + decoded(got_z[step - 1, m], size_z_in[step - 1, m, 0:1, :])
                 total[m, z, x, :, y] = acc
+                square_acc[...] = square_acc[...] + jnp.sum(acc * acc, axis=(0, 1)).reshape(1, cols)
 
             over(unit, body)
             push(lambda: core_copy(unit))
@@ -931,23 +951,22 @@
         mid_low[b] = back
         add_affine(8, column_sum(back.astype(F32)))
 
-    each(encode)
-    gathered(3, 2)
-    gathered(2, 3)
-    gathered(5, 1)
+    each(encode, hooks=(None, lambda: gather_step(4)))
+    gather_step(5)
 
     def first_project(b):
         project(0, b)
 
     each(first_project)
-    gathered(4, 2)
-    gathered(3, 3)
-    gathered(2, 4)
+    gather_step(6)
+    done = 7
     for layer in range(last):
 
         def attend_this(b, layer=layer):
+            attend(layer, b)
+
+        def take_first(b, layer=layer):
             take_prev(layer, b)
-            attend(layer, b)
 
         def mlp_this(b, layer=layer):
             mlp(layer, b)
@@ -955,30 +974,26 @@
         def project_next(b, layer=layer):
             project(layer + 1, b)
 
-        def ready(g=2 * layer):
-            gathered(5, g + 2)
-            gathered(4, g + 3)
-            gathered(3, g + 4)
-
-        def ready_next(g=2 * layer):
-            gathered(5, g + 3)
-            gathered(4, g + 4)
-
-        staggered(attend_this, mlp_this, project_next, hooks=(None, ready, ready_next))
-        gathered(2, 2 * layer + 5)
-        gathered(3, 2 * layer + 5)
-        gathered(2, 2 * layer + 6)
-        gathered(4, 2 * layer + 5)
-        gathered(3, 2 * layer + 6)
+        if layer > 0:
+            each(take_first)
+        staggered(
+            attend_this,
+            mlp_this,
+            project_next,
+            hooks=(None, lambda k=done: gather_step(k), lambda k=done + 1: gather_step(k)),
+        )
+        gather_step(done + 2)
+        done = done + 3
 
     def ready_last():
-        if last == 0:
-            gathered(4, 2)
-        gathered(5, 2 * last + 2)
+        for step in range(done, len(sz.groups) + 3):
+            gather_step(step)
         scalars[1] = tile_end(0) if sz.fused else jnp.broadcast_to(weight_ref[...], (8, 128))
 
+    def take_last(b):
+        take_prev(last, b)
+
     def attend_last(b):
-        take_prev(last, b)
         attend(last, b)
 
     def turn(b):
@@ -991,10 +1006,10 @@
         if last > 0:
             send_prev(last, b)
 
-    staggered(attend_last, turn, send_last, hooks=(None, ready_last))
+    staggered(take_last, attend_last, turn, send_last, hooks=(None, None, ready_last))
     outer_mlp(last)
+    outer_mixed(last)
     summed(1, 2 * last + 2)
-    outer_mixed(last)
     outer_pair(last)
     summed(1, 2 * last + 1)
     for layer in reversed(range(last)):
@@ -1002,8 +1017,6 @@
         def take_this(b, layer=layer):
             take_next(layer + 1, b)
 
-        each(take_this)
-
         def back_this(b, layer=layer):
             join(layer + 1, b)
             mlp_back(layer, b)
@@ -1016,8 +1029,11 @@
                 send_prev(layer, b)
 
         u = 2 * layer
-        each(back_this, hooks=(None, lambda u=u: summed(2, u + 4), lambda u=u: summed(2, u + 3)))
+        staggered(
+            take_this, back_this, hooks=(None, None, lambda u=u: summed(2, u + 4), lambda u=u: summed(2, u + 3))
+        )
         outer_mlp(layer)
+        outer_mixed(layer)
         summed(1, u + 2)
         summed(3, u + 4)
         hooks = (None, lambda u=u: summed(2, u + 2), lambda u=u: summed(3, u + 3))
@@ -1025,7 +1041,6 @@
             staggered(pair_this, send_this, hooks=hooks)
         else:
             each(pair_this, hooks=hooks)
-        outer_mixed(layer)
         outer_pair(layer)
         summed(1, u + 1)
         summed(4, u + 4)
@@ -1036,7 +1051,7 @@
         join(0, b)
         encode_back(b)
 
-    each(last_back, hooks=(None, lambda: summed(3, 2), lambda: summed(2, 1)))
+    each(last_back, hooks=(None, lambda: summed(3, 2)))
     wide = jnp.concatenate([affine_grad[...], jnp.zeros((112, width), F32)], axis=0)
 
     @pl.when(j == 0)
@@ -1064,25 +1079,21 @@
         reduce_one(0)
         if sz.layers > 1:
             reduce_four(3)
-        reduce_three(1)
+        reduce_two(1)
         reduce_two(0)
         reduce_four(2)
+        reduce_three(1)
         reduce_three(0)
         for unit in range(2, len(sz.units)):
             reduce_done(unit)
         reduce_four(1)
         reduce_four(0)
-        reduce_done(1)
-        reduce_done(0)
-        squares = jnp.zeros((1, 1), F32)
-        for index in range(sz.mats):
-            value = share[index]
-            squares = squares + jnp.sum(
-                jnp.sum(value * value, axis=1, keepdims=True), axis=0, keepdims=True
-            )
+        squares = jnp.sum(square_acc[...], axis=1, keepdims=True)
         sub = lax.broadcasted_iota(jnp.int32, (8, 128), 0)
         tile[1, 0] = jnp.where(sub == 0, squares, loss_acc[0:1, 0:1])
         tile_start(1)
+        reduce_done(1)
+        reduce_done(0)
         result = tile_end(1)
         scalars[0] = jnp.broadcast_to(result[1:2, :], (8, 128))
         scalars[2] = jnp.broadcast_to(jnp.sqrt(result[0:1, :]), (8, 128))
@@ -1119,6 +1130,8 @@
             pltpu.VMEM((sz.mats, sz.depth, 2, 2, 2, sz.shard, width), BF16),
             pltpu.VMEM((sz.mats, sz.depth, 2, 2, 2, sz.shard, cols), F32),
         ]
+        scratch += [pltpu.VMEM(value.shape, value.dtype) for value in operands]
+        scratch += [dma(len(operands))]
     else:
         out_shape = (
             jax.ShapeDtypeStruct((sz.mats, width, cols), F32),
@@ -1157,6 +1170,7 @@
         pltpu.VMEM((max(layers - 1, 1), nb, rows, cols), BF16),
         pltpu.VMEM((max(layers - 1, 1), nb, rows, width), BF16),
         pltpu.VMEM((8, 128), F32),
+        pltpu.VMEM((1, cols), F32),
     ]
     scratch += [dma(3), dma(3), dma(2), dma(2), dma(2), dma(2)] + [dma(layers, nb)] * 12
     scratch += [pltpu.SemaphoreType.REGULAR]
@@ -1185,7 +1199,7 @@
     return pl.pallas_call(
         functools.partial(step_kernel, sz),
         out_shape=out_shape,
-        in_specs=[pl.BlockSpec(memory_space=pltpu.VMEM)] * len(operands),
+        in_specs=[pl.BlockSpec(memory_space=pl.ANY if sz.fused else pltpu.VMEM)] * len(operands),
         out_specs=(pl.BlockSpec(memory_space=pltpu.VMEM),) * 2,
         scratch_shapes=scratch,
         compiler_params=pltpu.CompilerParams(
@@ -1206,6 +1220,8 @@
 def adam_kernel(sz, share, scalars, *refs):
     masters = refs[:15]
     outs = refs[15:35]
+    for index, ref in enumerate(refs[35:38]):
+        ref[...] = scalars[index, 0:1, 0:1]
     mat, inp, out, gain, bias = [masters[3 * k : 3 * k + 3] for k in range(5)]
     factor = jnp.minimum(1.0, CLIP / (scalars[2, 0:1, 0:1] + 1e-06))
 
@@ -1234,6 +1250,7 @@
         operands += list(triple)
         shape = triple[0].shape
         out_shape += [jax.ShapeDtypeStruct(shape, F32)] * 3 + [jax.ShapeDtypeStruct(shape, BF16)]
+    out_shape += [jax.ShapeDtypeStruct((1, 1), F32)] * 3
     return pl.pallas_call(
         functools.partial(adam_kernel, sz),
         out_shape=tuple(out_shape),
@@ -1264,7 +1281,7 @@
         jnp.swapaxes(grid_in, 1, 2),
         jnp.swapaxes(targets, 1, 2),
         area.reshape(1, -1),
-        row_count,
+        row_count.T,
         g2m.T,
         m2g.T,
         senders.T,
@@ -1283,7 +1300,9 @@
         outs = list(update(sz, share, scalars, groups))
         for index in range(4, 8):
             outs[index] = outs[index].T
-        return tuple(outs) + (scalars[0, 0, 0], scalars[1, 0, 0], scalars[2, 0, 0])
+        for index in range(20, 23):
+            outs[index] = outs[index].reshape(())
+        return tuple(outs)
 
     width, shard = sz.width, sz.shard
 

time: 163 us -> 147 us (0.902)
  Pallas kernels: 159 us -> 146 us
  local copies, waits for them, and re-layouts: 2.52 us -> 0 us
    pallas_call x1, Pallas kernels: 156 us -> 143 us  [train_kernel(): pl.pallas_call(functools.partial(step_kernel, sz), out_shape=out_shape, i...]
where the time goes in v3:
time: 147 us
  Pallas kernels  146 us (99%)
    pallas_call x1, Pallas kernels, train_kernel(): pl.pallas_call(functools.partial(step_kernel, sz), out_shape=out_shape, i...  143 us
    pallas_call x1, Pallas kernels, update(): pl.pallas_call(functools.partial(adam_kernel, sz), out_shape=tuple(out_sh...  2.95 us

profile of v3, /device:TPU:0, one launch (start us, length us, event | category | flops | bytes accessed | tf_op | source)
XLA Modules:
  0.0 146.9 jit_solution(12991531585578065197)
XLA Ops:
  0.7 143.2 %shard_map.398 = (f32[13,16,512]{2,1,0:T(8,128)}, f32[3,8,128]{2,1,0:T(8,128)}) custom-call(bf16[3,227,128]{2,1,0:T(8,128)(2,1)} %bitcast.18, bf16[3,83,128]{2,1,0:T(8,128)(2,1)} %bitcast.19, f32[1,128]{1,0:T(1,128)} %bitcast.27, s32[1,3]{1,0:T(1,128)} %bitcast.28, s32[8,256]{1,0:T(8,128)} %bitcast.25, s32[3,256]{1,0:T(4,128)} %bitcast.26, ...), custom_call_target="tpu_custom_call" | custom-call | tf_op jit(solution)/shard_map/pallas_call | solution.py:1199
  143.8 2.9 %shard_map.399 = (f32[12,16,512]{2,1,0:T(8,128)}, f32[12,16,512]{2,1,0:T(8,128)}, f32[12,16,512]{2,1,0:T(8,128)}, bf16[12,16,512]{2,1,0:T(8,128)(2,1)}, f32[16,2...) custom-call(f32[13,16,512]{2,1,0:T(8,128)} %get-tuple-element.48.sha, ...), custom_call_target="tpu_custom_call" | custom-call | tf_op jit(solution)/shard_map/pallas_call | solution.py:1254

commit v4 on v3

--- a/solution.py
+++ b/solution.py
@@ -609,7 +609,7 @@
             score = nt(queries * mask_low[head], keys) * scale + edge_bias[...]
             expo = jnp.exp(score - jnp.max(score, axis=-1, keepdims=True))
             weight = (expo * (1.0 / jnp.sum(expo, axis=-1, keepdims=True))).astype(BF16)
-            prob[layer, b, head] = weight
+            prob[spot(layer, b), head] = weight
             out = out + nn(weight, values) * mask_full[head]
         mixed[layer, b, j] = out.astype(BF16)
         mix_copy(layer, b).start()
@@ -848,17 +848,19 @@
         grad_out = nt(mid_low[b], w_rows(base + 3, j)).astype(BF16)
         keys, values, queries = pair[layer, b, 0], pair[layer, b, 1], query[layer, b]
         d_query = jnp.zeros((rows, cols), F32)
-        d_keys = jnp.zeros((2 * rows, cols), F32)
-        d_values = jnp.zeros((2 * rows, cols), F32)
+        scores = []
+        out_heads = jnp.concatenate([grad_out * mask for mask in mask_low], axis=0)
+        query_heads = jnp.concatenate([queries * mask for mask in mask_low], axis=0)
         for head in range(sz.near):
-            weight_low = prob[layer, b, head]
-            out_head = grad_out * mask_low[head]
+            weight_low = prob[spot(layer, b), head]
+            out_head = out_heads[head * rows : (head + 1) * rows]
             weight = weight_low.astype(F32)
             part = weight * nt(out_head, values)
             score = (part - weight * jnp.sum(part, axis=-1, keepdims=True)).astype(BF16)
             d_query = d_query + nn(score, keys) * mask_full[head]
-            d_keys = d_keys + tn(score, queries * mask_low[head])
-            d_values = d_values + tn(weight_low, out_head)
+            scores.append(score)
+        d_keys = tn(jnp.concatenate(scores, axis=0), query_heads)
+        d_values = tn(prob[spot(layer, b)].reshape(sz.near * rows, 2 * rows), out_heads)
         d_keys = (d_keys * scale).astype(BF16)
         d_values = d_values.astype(BF16)
         d_own[b, :, 0:cols] = (d_query * scale).astype(BF16)
@@ -1030,19 +1032,20 @@
 
         u = 2 * layer
         staggered(
-            take_this, back_this, hooks=(None, None, lambda u=u: summed(2, u + 4), lambda u=u: summed(2, u + 3))
+            take_this, back_this, hooks=(None, None, None, lambda u=u: summed(2, u + 4))
         )
         outer_mlp(layer)
         outer_mixed(layer)
         summed(1, u + 2)
-        summed(3, u + 4)
-        hooks = (None, lambda u=u: summed(2, u + 2), lambda u=u: summed(3, u + 3))
+        summed(2, u + 3)
+        hooks = (None, lambda u=u: summed(3, u + 4), lambda u=u: summed(2, u + 2))
         if layer > 0:
             staggered(pair_this, send_this, hooks=hooks)
         else:
             each(pair_this, hooks=hooks)
         outer_pair(layer)
         summed(1, u + 1)
+        summed(3, u + 3)
         summed(4, u + 4)
         if layer > 0:
             summed(4, u + 3)
@@ -1077,13 +1080,13 @@
 
     if sz.fused:
         reduce_one(0)
+        reduce_two(1)
+        reduce_two(0)
         if sz.layers > 1:
             reduce_four(3)
-        reduce_two(1)
-        reduce_two(0)
-        reduce_four(2)
         reduce_three(1)
         reduce_three(0)
+        reduce_four(2)
         for unit in range(2, len(sz.units)):
             reduce_done(unit)
         reduce_four(1)
@@ -1150,7 +1153,7 @@
         pltpu.VMEM((layers, nb, 2, rows, cols), BF16),
         pltpu.VMEM((layers, nb, rows, cols), BF16),
         pltpu.VMEM((layers, nb, 2, 2 * rows, cols), BF16),
-        pltpu.VMEM((layers, nb, sz.near, rows, 2 * rows), BF16),
+        pltpu.VMEM(((layers - 1) * nb + 1, sz.near, rows, 2 * rows), BF16),
         pltpu.VMEM((rows, 2 * rows), F32),
     ]
     scratch += [pltpu.VMEM((rows, rows), BF16)] * 6

time: 147 us -> 142 us (0.966)
  Pallas kernels: 146 us -> 141 us
    pallas_call x1, Pallas kernels: 143 us -> 138 us  [train_kernel(): pl.pallas_call(functools.partial(step_kernel, sz), out_shape=out_shape, i...]
where the time goes in v4:
time: 142 us
  Pallas kernels  141 us (99%)
    pallas_call x1, Pallas kernels, train_kernel(): pl.pallas_call(functools.partial(step_kernel, sz), out_shape=out_shape, i...  138 us
    pallas_call x1, Pallas kernels, update(): pl.pallas_call(functools.partial(adam_kernel, sz), out_shape=tuple(out_sh...  2.95 us

profile of v4, /device:TPU:0, one launch (start us, length us, event | category | flops | bytes accessed | tf_op | source)
XLA Modules:
  0.0 141.9 jit_solution(2053054401192030107)
XLA Ops:
  0.7 138.1 %shard_map.398 = (f32[13,16,512]{2,1,0:T(8,128)}, f32[3,8,128]{2,1,0:T(8,128)}) custom-call(bf16[3,227,128]{2,1,0:T(8,128)(2,1)} %bitcast.18, bf16[3,83,128]{2,1,0:T(8,128)(2,1)} %bitcast.19, f32[1,128]{1,0:T(1,128)} %bitcast.27, s32[1,3]{1,0:T(1,128)} %bitcast.28, s32[8,256]{1,0:T(8,128)} %bitcast.25, s32[3,256]{1,0:T(4,128)} %bitcast.26, ...), custom_call_target="tpu_custom_call" | custom-call | tf_op jit(solution)/shard_map/pallas_call | solution.py:1202
  138.7 2.9 %shard_map.399 = (f32[12,16,512]{2,1,0:T(8,128)}, f32[12,16,512]{2,1,0:T(8,128)}, f32[12,16,512]{2,1,0:T(8,128)}, bf16[12,16,512]{2,1,0:T(8,128)(2,1)}, f32[16,2...) custom-call(f32[13,16,512]{2,1,0:T(8,128)} %get-tuple-element.48.sha, ...), custom_call_target="tpu_custom_call" | custom-call | tf_op jit(solution)/shard_map/pallas_call | solution.py:1257
